TPU v7x, 32 devices: a whole 2x2x4 slice. The times are simulated.
32 devices in a mesh: expert: 8 (over y, x, core), hidden: 4 (over z).
Axes of the slice: x: 2, y: 2, z: 4, core: 2. Of those that a mesh axis runs over, the one named last changes fastest.
Arguments:
- tokens: bfloat16 [8192, 1024], P(('expert', 'hidden')), may hold values from -6 to 6
- assignment: int32 [8192, 1], P(('expert', 'hidden')), may hold values from 0 to 15; in each aligned block of 256 rows (0 to 255, 256 to 511, ...) at most 18 rows name the same one
- lengths: int32 [8], replicated, may hold values from 32 to 1024
- centroids: bfloat16 [16, 1024], P('expert', 'hidden'), may hold values from -0.125 to 0.125
- ln_gain: float32 [16, 1024], P('expert', 'hidden'), may hold values from 0.5 to 1.5
- ln_bias: float32 [16, 1024], P('expert', 'hidden'), may hold values from -2 to 2
- w_in: bfloat16 [16, 1024, 4096], P('expert', None, 'hidden'), may hold values from -0.1875 to 0.1875
- b_in: float32 [16, 4096], P('expert', 'hidden'), may hold values from -2 to 2
- w_out: bfloat16 [16, 4096, 1024], P('expert', 'hidden'), may hold values from -0.1875 to 0.1875
- b_out: float32 [16, 1024], P('expert', 'hidden'), may hold values from -2 to 2
- cotangent: bfloat16 [8192, 1024], P(('expert', 'hidden')), may hold values from -6 to 6
Outputs:
- mixed: bfloat16 [8192, 1024], P(('expert', 'hidden'))
- tokens_grad: bfloat16 [8192, 1024], P(('expert', 'hidden'))
- centroids_grad: float32 [16, 1024], P('expert', 'hidden')
- ln_gain_grad: float32 [16, 1024], P('expert', 'hidden')
- ln_bias_grad: float32 [16, 1024], P('expert', 'hidden')
- w_in_grad: float32 [16, 1024, 4096], P('expert', None, 'hidden')
- b_in_grad: float32 [16, 4096], P('expert', 'hidden')
- w_out_grad: float32 [16, 4096, 1024], P('expert', 'hidden')
- b_out_grad: float32 [16, 1024], P('expert', 'hidden')
- mean_gate: float32 [16], replicated
Inputs may be any that keep to these rules, and one draw needn't show every extreme that they name: `assignment`: in each aligned block of 256 rows (the rows of one device) no expert is named by more than 18 rows, a bound that some block reaches; every expert is named by some row.
All inputs are finite; a program needn't handle non-finite values.
Results may differ from a plain program's by a relative error of at most 0.0061.
Values may be sent and summed in bfloat16 or wider, within the bound.
A program may use at most 128 MiB of HBM per device.

v0:
```python
import jax
import jax.numpy as jnp
from jax import lax
from jax.sharding import PartitionSpec as P

EPS = 1e-05
HIGH = lax.Precision.HIGHEST


def spread_rows(buffer):
    shared = lax.all_gather(buffer, "hidden", axis=0, tiled=True)
    return lax.all_to_all(shared, "expert", split_axis=1, concat_axis=1, tiled=True)


def send_home(buffer):
    return lax.all_to_all(buffer, "expert", split_axis=1, concat_axis=1, tiled=True)


def standardize(rows):
    mean = jnp.mean(rows, axis=-1, keepdims=True)
    centered = rows - mean
    var = jnp.mean(centered * centered, axis=-1, keepdims=True)
    factor = lax.rsqrt(var + EPS)
    return (centered * factor, factor)


def on_device(
    tokens, assignment, lengths, centroids, ln_gain, ln_bias, w_in, b_in, w_out, b_out, cotangent
):
    tok_dev, width = tokens.shape
    groups = lax.axis_size("expert")
    hidden_count = lax.axis_size("hidden")
    exp_dev = w_in.shape[0]
    experts = exp_dev * groups
    slots = max(2, 9 * tok_dev // (8 * experts))
    seq_len = min(2048, hidden_count * tok_dev)
    part_width = centroids.shape[1]
    place = lax.axis_index(("expert", "hidden"))
    hidden_place = lax.axis_index("hidden")
    position = place * tok_dev + jnp.arange(tok_dev, dtype=jnp.int32)
    live = position % seq_len < jnp.take(lengths, position // seq_len)
    livef = live.astype(jnp.float32)
    chosen = assignment[:, 0]
    onehot = (
        (chosen[:, None] == jnp.arange(experts, dtype=jnp.int32)[None, :]) & live[:, None]
    ).astype(jnp.int32)
    before = jnp.cumsum(onehot, axis=0) - onehot
    rank = jnp.sum(before * onehot, axis=1)
    target = jnp.where(live, chosen * slots + rank, experts * slots)
    dispatch = (target[None, :] == jnp.arange(experts * slots, dtype=jnp.int32)[:, None]).astype(
        jnp.bfloat16
    )
    hot = onehot.astype(jnp.float32)
    centre_flat = lax.all_gather(centroids.reshape(-1), ("expert", "hidden"), axis=0, tiled=True)
    cent_all = (
        centre_flat.reshape(groups, hidden_count, exp_dev, part_width)
        .transpose(0, 2, 1, 3)
        .reshape(experts, width)
    )
    home_rows = jnp.dot(dispatch, tokens, preferred_element_type=jnp.float32).astype(jnp.bfloat16)
    home_buffer = home_rows.reshape(1, groups, exp_dev, slots, width)
    gain_all, shift_all, bias_out_all = (
        lax.all_gather(ln_gain, "hidden", axis=1, tiled=True),
        lax.all_gather(ln_bias, "hidden", axis=1, tiled=True),
        lax.all_gather(b_out, "hidden", axis=1, tiled=True),
    )
    expert_rows = spread_rows(home_buffer)
    normed, _ = standardize(expert_rows.astype(jnp.float32))
    lifted = (normed * gain_all[:, None, :] + shift_all[:, None, :]).astype(jnp.bfloat16)
    pre = (
        jnp.einsum("hgjcd,jdf->hgjcf", lifted, w_in, preferred_element_type=jnp.float32)
        + b_in[:, None, :]
    )
    active = jax.nn.gelu(pre).astype(jnp.bfloat16)
    piece = active
    summed = lax.psum_scatter(
        jnp.einsum("hgjcf,jfd->hgjcd", piece, w_out, preferred_element_type=jnp.float32),
        "hidden",
        scatter_dimension=0,
        tiled=True,
    )
    branch_rows = (summed + bias_out_all[:, None, :]).astype(jnp.bfloat16)
    returned = send_home(branch_rows).reshape(experts * slots, width)
    branch = jnp.dot(dispatch.T, returned, preferred_element_type=jnp.float32)
    scores = jnp.dot(tokens, cent_all.T, preferred_element_type=jnp.float32)
    score = jnp.sum(scores * hot, axis=1)
    gate = jax.nn.sigmoid(score) * livef
    mixed = (tokens.astype(jnp.float32) + gate[:, None] * branch).astype(jnp.bfloat16)
    gate_sum, live_count = lax.psum(
        (jnp.sum(hot * gate[:, None], axis=0), jnp.sum(hot, axis=0)), ("expert", "hidden")
    )
    mean_gate = gate_sum / jnp.maximum(live_count, 1.0)
    upstream = cotangent.astype(jnp.float32)
    branch_grad = (gate[:, None] * upstream).astype(jnp.bfloat16)
    gate_grad = jnp.sum(upstream * branch, axis=1)
    score_grad = gate_grad * gate * (1.0 - gate)
    grad_home = jnp.dot(dispatch, branch_grad, preferred_element_type=jnp.float32).astype(
        jnp.bfloat16
    )
    grad_buffer = grad_home.reshape(1, groups, exp_dev, slots, width)
    grad_rows = spread_rows(grad_buffer)
    own_grad = lax.dynamic_index_in_dim(grad_rows, hidden_place, 0, keepdims=False).astype(
        jnp.float32
    )
    bias_out_grad = jnp.sum(own_grad, axis=(0, 2))
    act_grad = jnp.einsum("hgjcd,jfd->hgjcf", grad_rows, w_out, preferred_element_type=jnp.float32)
    w_out_grad = jnp.einsum(
        "hgjcf,hgjcd->jfd", active, grad_rows, preferred_element_type=jnp.float32
    )
    pre_grad = jax.vjp(jax.nn.gelu, pre)[1](act_grad)[0].astype(jnp.bfloat16)
    b_in_grad = jnp.sum(pre_grad.astype(jnp.float32), axis=(0, 1, 3))
    w_in_grad = jnp.einsum("hgjcd,hgjcf->jdf", lifted, pre_grad, preferred_element_type=jnp.float32)
    piece = pre_grad
    lifted_grad = lax.psum_scatter(
        jnp.einsum("hgjcf,jdf->hgjcd", piece, w_in, preferred_element_type=jnp.float32),
        "hidden",
        scatter_dimension=0,
        tiled=True,
    )[0]
    own_rows = lax.dynamic_index_in_dim(expert_rows, hidden_place, 0, keepdims=False).astype(
        jnp.float32
    )
    own_normed, own_factor = standardize(own_rows)
    gain_grad = jnp.sum(lifted_grad * own_normed, axis=(0, 2))
    shift_grad = jnp.sum(lifted_grad, axis=(0, 2))
    normed_grad = lifted_grad * gain_all[:, None, :]
    rows_grad = own_factor * (
        normed_grad
        - jnp.mean(normed_grad, axis=-1, keepdims=True)
        - own_normed * jnp.mean(normed_grad * own_normed, axis=-1, keepdims=True)
    )
    back_rows = send_home(rows_grad.astype(jnp.bfloat16)[None]).reshape(experts * slots, width)
    token_back = jnp.dot(dispatch.T, back_rows, preferred_element_type=jnp.float32)
    cent_tok = jnp.dot(onehot.astype(jnp.bfloat16), cent_all, preferred_element_type=jnp.float32)
    tokens_grad = (upstream + score_grad[:, None] * cent_tok + token_back).astype(jnp.bfloat16)
    gain_part, shift_part, bias_part = (
        lax.psum_scatter(gain_grad, "hidden", scatter_dimension=1, tiled=True),
        lax.psum_scatter(shift_grad, "hidden", scatter_dimension=1, tiled=True),
        lax.psum_scatter(bias_out_grad, "hidden", scatter_dimension=1, tiled=True),
    )
    cent_local = jnp.dot((hot * score_grad[:, None]).T, tokens.astype(jnp.float32), precision=HIGH)
    arranged = (
        cent_local.reshape(groups, exp_dev, hidden_count, part_width)
        .transpose(0, 2, 1, 3)
        .reshape(-1)
    )
    cent_grad = lax.psum_scatter(
        arranged, ("expert", "hidden"), scatter_dimension=0, tiled=True
    ).reshape(exp_dev, part_width)
    return (
        mixed,
        tokens_grad,
        cent_grad,
        gain_part,
        shift_part,
        w_in_grad,
        b_in_grad,
        w_out_grad,
        bias_part,
        mean_gate,
    )


def solution(mesh):
    in_specs = (
        P(("expert", "hidden"), None),
        P(("expert", "hidden"), None),
        P(),
        P("expert", "hidden"),
        P("expert", "hidden"),
        P("expert", "hidden"),
        P("expert", None, "hidden"),
        P("expert", "hidden"),
        P("expert", "hidden", None),
        P("expert", "hidden"),
        P(("expert", "hidden"), None),
    )
    out_specs = (
        P(("expert", "hidden"), None),
        P(("expert", "hidden"), None),
        P("expert", "hidden"),
        P("expert", "hidden"),
        P("expert", "hidden"),
        P("expert", None, "hidden"),
        P("expert", "hidden"),
        P("expert", "hidden", None),
        P("expert", "hidden"),
        P(),
    )
    return jax.shard_map(
        on_device, mesh=mesh, in_specs=in_specs, out_specs=out_specs, check_vma=False
    )
```

profile of v0, /device:TPU:0, one launch (start us, length us, event | category | flops | bytes accessed | tf_op | source)
XLA Modules:
  0.0 654.7 jit_solution(1662345047142384501)
XLA Ops:
  7.3 1.6 fusion.81
  8.8 4.5 compare_select_fusion.1
  14.7 0.7 fusion.72
  16.2 0.8 fusion.65
  17.0 0.7 add_select_fusion
  17.7 1.4 convolution_convert_fusion.1
  19.2 1.1 copy.87
  20.4 53.3 %all-gather.4.cloned.1.call-done = bf16[4,8,2,18,1024]{4,1,3,2,0:T(8,128)(2,1)} async-done(((bf16[1,8,2,18,1024]{4,1,3,2,0:T(8,128)(2,1)}), bf16[4,8,2,18,1024]{4,1,3,2,0:T(8,128)(2,1)}) %all-gather.4.cloned.1.call-update) | async-done | bytes 2359312 | tf_op jit(solution)/shard_map/all_gather | solution.py:11
  73.7 4.9 copy.88
  78.6 3.8 all-to-all-start
  82.4 11.9 %all_gather.21 = f32[2,1024]{1,0:T(2,128)S(1)} all-gather(f32[2,256]{1,0:T(2,128)S(1)} %copy-done.7), channel_id=1, replica_groups=mesh['expert'=8,'hidden'=4] {'hidden'}, dimensions={1}, use_global_device_ids=true | all-gather | bytes 10240 | tf_op jit(solution)/shard_map/all_gather | solution.py:64
  94.3 11.9 %all_gather.20 = f32[2,1024]{1,0:T(2,128)S(1)} all-gather(f32[2,256]{1,0:T(2,128)S(1)} %copy-done.8), channel_id=1, replica_groups=mesh['expert'=8,'hidden'=4] {'hidden'}, dimensions={1}, use_global_device_ids=true | all-gather | bytes 10240 | tf_op jit(solution)/shard_map/all_gather | solution.py:63
  106.2 5.7 all-to-all-done
  111.8 1.0 convert_reduce_fusion.1
  112.9 1.7 fusion.13
  114.6 2.2 fusion.16
  116.9 7.4 %fusion.10 = (bf16[4,8,2,18,1024]{4,3,1,0,2:T(8,128)(2,1)S(1)}, f32[2,4,8,18,1024]{4,3,2,1,0:T(8,128)}) fusion(f32[2,1024]{1,0:T(2,128)S(1)} %copy-done.14, bf16[2,1024,1024]{2,1,0:T(8,128)(2,1)S(1)} %copy-done.12, bf16[4,8,2,18,1024]{4,0,3,2,1:T(4,128)(2,1)S(1)} %fusion.16), kind=kOutput, calls=%fused_computation.15 | convolution fusion | flops 2427715584 | bytes 13639680 | tf_op jit(solution)/shard_map/hgjcd,jdf->hgjcf/dot_general | solution.py:71
  124.2 3.5 fusion.30
  127.7 4.9 copy.90
  133.3 12.1 %all_gather.22 = f32[2,1024]{1,0:T(2,128)S(1)} all-gather(f32[2,256]{1,0:T(2,128)S(1)} %copy-done.9), channel_id=1, replica_groups=mesh['expert'=8,'hidden'=4] {'hidden'}, dimensions={1}, use_global_device_ids=true | all-gather | bytes 10240 | tf_op jit(solution)/shard_map/all_gather | solution.py:65
  145.4 69.8 %reduce-scatter.12.cloned.1.call-done = f32[1,8,2,18,1024]{4,1,3,2,0:T(8,128)} async-done(((f32[4,8,2,18,1024]{4,1,3,2,0:T(8,128)}), f32[1,8,2,18,1024]{4,1,3,2,0:T(8,128)}) %reduce-scatter.12.cloned.1.call-update) | async-done | bytes 1179664 | tf_op jit(solution)/shard_map/reduce_scatter | solution.py:76
  215.1 1.4 add_convert_fusion
  216.5 1.4 copy.91
  217.9 4.2 all-to-all-start.1
  222.2 68.8 %all-gather = bf16[32,1,512]{2,1,0:T(2,128)(2,1)S(1)} all-gather(bf16[1,1,512]{2,1,0:T(2,128)(2,1)S(1)} %reshape.318), channel_id=1, replica_groups=mesh['expert'=8,'hidden'=4] {'expert','hidden'}, dimensions={0}, use_global_device_ids=true | all-gather | bytes 33792 | tf_op jit(solution)/shard_map/all_gather | solution.py:54
  291.5 2.1 copy.92
  293.7 2.1 reshape.276
  295.8 2.5 fusion.52
  298.3 1.2 convolution_convert_fusion
  299.6 2.1 reshape.277
  301.7 2.3 copy.94
  304.0 47.1 %all-gather.6.cloned.1.call-done = bf16[4,8,2,18,1024]{4,1,3,2,0:T(8,128)(2,1)} async-done(((bf16[1,8,2,18,1024]{4,1,3,2,0:T(8,128)(2,1)}), bf16[4,8,2,18,1024]{4,1,3,2,0:T(8,128)(2,1)}) %all-gather.6.cloned.1.call-update) | async-done | bytes 2359312 | tf_op jit(solution)/shard_map/all_gather | solution.py:11
  351.1 4.9 copy.95
  356.0 4.4 all-to-all-start.2
  360.4 1.0 fusion.66
  361.3 0.9 reshape.279
  363.0 27.0 %all-to-all-done.2 = bf16[4,8,2,18,1024]{4,0,3,2,1:T(4,128)(2,1)} async-done(((bf16[4,8,2,18,1024]{4,0,3,2,1:T(4,128)(2,1)}), bf16[4,8,2,18,1024]{4,0,3,2,1:T(4,128)(2,1)}, u32[]{:S(2)}, u32[]{:S(2)}) %all-to-all-start.2) | async-done | bytes 2359328 | tf_op jit(solution)/shard_map/all_to_all | solution.py:12
  390.0 11.9 %convert_reduce_fusion = (f32[2,1024]{1,0:T(2,128)}, bf16[4,8,2,18,1024]{4,3,1,0,2:T(8,128)(2,1)S(1)}) fusion(f32[2,4,8,18,1024]{4,3,2,1,0:T(8,128)} %get-tuple-element.32, f32[2,1024]{1,0:T(2,128)S(1)} %copy-done.14, bf16[2,1024,1024]{2,1,0:T(8,128)(2,1)} %param.19, bf16[4,8,2,18,1024]{4,0,3,2,1:T(4,128)(2,1)} %all-to-all-done.2), kind=kOutput, calls=%fused_computation.16 | convolution fusion | flops 2443048960 | bytes 13647872 | tf_op jit(solution)/shard_map/hgjcd,jfd->hgjcf/dot_general | solution.py:106
  402.0 3.5 fusion.33
  405.5 4.9 copy.97
  410.6 1.2 constant_dynamic-slice_fusion
  411.8 0.8 convert_reduce_fusion.2
  413.0 38.2 %all-reduce.1 = (f32[16]{0:T(128)S(1)}, f32[16]{0:T(128)S(1)}) all-reduce(f32[16]{0:T(128)S(1)} %get-tuple-element.14, f32[16]{0:T(128)S(1)} %get-tuple-element.13), channel_id=1, replica_groups=mesh['expert'=8,'hidden'=4] {'expert','hidden'}, use_global_device_ids=true, to_apply=%region_22.23 | all-reduce | flops 32 | bytes 256 | tf_op jit(solution)/shard_map/psum | solution.py:89
  451.7 1.3 convert_add_fusion
  453.1 1.0 add_convert_fusion.1
  454.1 32.2 %all-reduce.4.cloned.1.call-done = f32[16384]{0:T(1024)} async-done(((f32[16384]{0:T(1024)}), f32[16384]{0:T(1024)}) %all-reduce.4.cloned.1.call-update) | async-done | bytes 65552
  486.3 0.7 dynamic-slice
  487.6 3.2 convert_reduce_fusion.3
  490.8 1.1 copy.113
  491.9 9.8 %convolution_bitcast_fusion.1 = f32[2,1024,1024]{2,1,0:T(8,128)} fusion(bf16[4,8,2,18,1024]{4,3,1,0,2:T(8,128)(2,1)} %copy-done.16, bf16[4,8,2,18,1024]{4,0,3,2,1:T(4,128)(2,1)} %copy-done.5), kind=kOutput, calls=%fused_computation.33 | convolution fusion | flops 2415919104 | bytes 13107200 | tf_op jit(solution)/shard_map/hgjcd,hgjcf->jdf/dot_general | solution.py:112
  501.7 73.4 %reduce-scatter.14.cloned.1.call-done = f32[1,8,2,18,1024]{4,1,3,2,0:T(8,128)} async-done(((f32[4,8,2,18,1024]{4,1,3,2,0:T(8,128)}), f32[1,8,2,18,1024]{4,1,3,2,0:T(8,128)}) %reduce-scatter.14.cloned.1.call-update) | async-done | bytes 1179664 | tf_op jit(solution)/shard_map/reduce_scatter | solution.py:114
  575.1 1.9 fusion.43
  577.0 1.0 copy.109
  578.5 1.4 copy.98
  580.0 3.7 all-to-all-start.3
  583.9 1.0 copy.111
  584.9 9.9 %convolution_bitcast_fusion = f32[2,1024,1024]{2,1,0:T(8,128)} fusion(bf16[4,8,2,18,1024]{4,0,3,2,1:T(4,128)(2,1)} %all-to-all-done.2, bf16[4,8,2,18,1024]{4,3,1,0,2:T(8,128)(2,1)} %copy-done.15), kind=kOutput, calls=%fused_computation.32 | convolution fusion | flops 2415919104 | bytes 13107200 | tf_op jit(solution)/shard_map/hgjcf,hgjcd->jfd/dot_general | solution.py:107
  594.9 4.6 reduce-scatter.20.cloned.1.call-done
  599.4 1.6 copy.114
  601.0 21.2 %reduce-scatter.16.cloned.1.call-done = f32[256,2]{1,0:T(8,128)} async-done(((f32[1024,2]{1,0:T(8,128)}), f32[256,2]{1,0:T(8,128)}) %reduce-scatter.16.cloned.1.call-update) | async-done | bytes 2064
  622.2 1.6 copy.110
  623.8 20.6 %reduce-scatter.18.cloned.1.call-done = f32[256,2]{1,0:T(8,128)} async-done(((f32[1024,2]{1,0:T(8,128)}), f32[256,2]{1,0:T(8,128)}) %reduce-scatter.18.cloned.1.call-update) | async-done | bytes 2064
  644.4 1.6 copy.112
  646.3 1.3 fusion.36
  (81 shorter events, 7.5 us)
Async XLA Ops:
  7.2 66.5 %all-gather.4.cloned.1.call-start = ((), (), s32[]{:S(2)}) async-start(), calls=%async_computation.9 | async-start | bytes 2949120 | tf_op jit(solution)/shard_map/all_gather | solution.py:11
  78.6 3.8 copy-start.7
  78.6 15.7 %copy-start.8 = (f32[2,256]{1,0:T(2,128)S(1)}, f32[2,256]{1,0:T(2,128)}, u32[]{:S(2)}) copy-start(f32[2,256]{1,0:T(2,128)} %param.15) | copy-start | bytes 6148
  78.6 33.2 %all-to-all-start = ((bf16[4,8,2,18,1024]{4,0,3,2,1:T(4,128)(2,1)}), bf16[4,8,2,18,1024]{4,0,3,2,1:T(4,128)(2,1)S(1)}, u32[]{:S(2)}, u32[]{:S(2)}) async-start(bf16[4,8,2,18,1024]{4,0,3,2,1:T(4,128)(2,1)} %copy.88), calls=%async_computation | async-start | bytes 4718592 | tf_op jit(solution)/shard_map/all_to_all | solution.py:12
  82.4 132.7 %reduce-scatter.12.cloned.1.call-start = ((), (), s32[]{:S(2)}) async-start(), calls=%async_computation.10 | async-start | bytes 5898240 | tf_op jit(solution)/shard_map/reduce_scatter | solution.py:76
  114.5 2.3 copy-start.12
  114.6 2.3 copy-start.14
  116.9 7.4 %copy-start.5 = (bf16[4,8,2,18,1024]{4,0,3,2,1:T(4,128)(2,1)}, bf16[4,8,2,18,1024]{4,0,3,2,1:T(4,128)(2,1)S(1)}, u32[]{:S(2)}) copy-start(bf16[4,8,2,18,1024]{4,0,3,2,1:T(4,128)(2,1)S(1)} %fusion.16) | copy-start | bytes 7077892
  116.9 7.4 %copy-start.11 = (bf16[2,1024,1024]{2,1,0:T(8,128)(2,1)S(1)}, bf16[2,1024,1024]{2,1,0:T(8,128)(2,1)}, u32[]{:S(2)}) copy-start(bf16[2,1024,1024]{2,1,0:T(8,128)(2,1)} %param.19) | copy-start | bytes 12582916
  124.2 3.5 copy-start.15
  132.6 0.7 copy-start.9
  133.3 88.9 %copy-start.10 = (bf16[2,256]{1,0:T(2,128)(2,1)S(1)}, bf16[2,256]{1,0:T(2,128)(2,1)}, u32[]{:S(2)}) copy-start(bf16[2,256]{1,0:T(2,128)(2,1)} %param.14) | copy-start | bytes 3076
  133.3 158.0 %copy-start = (bf16[256,1024]{1,0:T(8,128)(2,1)S(1)}, bf16[256,1024]{1,0:T(8,128)(2,1)}, u32[]{:S(2)}) copy-start(bf16[256,1024]{1,0:T(8,128)(2,1)} %param.11) | copy-start | bytes 1572868
  133.3 158.0 %copy-start.6 = (s32[256,1]{0,1:T(1,128)S(1)}, s32[256,1]{0,1:T(1,128)}, u32[]{:S(2)}) copy-start(s32[256,1]{0,1:T(1,128)} %param.12) | copy-start | bytes 3076
  216.5 79.3 %copy-start.1 = (bf16[256,1024]{1,0:T(8,128)(2,1)S(1)}, bf16[256,1024]{1,0:T(8,128)(2,1)}, u32[]{:S(2)}) copy-start(bf16[256,1024]{1,0:T(8,128)(2,1)} %param.21) | copy-start | bytes 1572868
  217.9 73.6 %all-to-all-start.1 = ((bf16[1,8,2,18,1024]{4,2,3,0,1:T(2,128)(2,1)}), bf16[1,8,2,18,1024]{4,2,3,0,1:T(2,128)(2,1)}, u32[]{:S(2)}, u32[]{:S(2)}) async-start(bf16[1,8,2,18,1024]{4,2,3,0,1:T(2,128)(2,1)} %copy.91), calls=%async_computation.2 | async-start | bytes 1179648 | tf_op jit(solution)/shard_map/all_to_all | solution.py:16
  222.2 128.9 %all-gather.6.cloned.1.call-start = ((), (), s32[]{:S(2)}) async-start(), calls=%async_computation.11 | async-start | bytes 2949120 | tf_op jit(solution)/shard_map/all_gather | solution.py:11
  356.0 34.1 %all-to-all-start.2 = ((bf16[4,8,2,18,1024]{4,0,3,2,1:T(4,128)(2,1)}), bf16[4,8,2,18,1024]{4,0,3,2,1:T(4,128)(2,1)}, u32[]{:S(2)}, u32[]{:S(2)}) async-start(bf16[4,8,2,18,1024]{4,0,3,2,1:T(4,128)(2,1)} %copy.95), calls=%async_computation.3 | async-start | bytes 4718592 | tf_op jit(solution)/shard_map/all_to_all | solution.py:12
  360.3 125.9 %all-reduce.4.cloned.1.call-start = ((), (), s32[]{:S(2)}) async-start(), calls=%async_computation.16 | async-start | bytes 131072
  362.9 212.1 %reduce-scatter.14.cloned.1.call-start = ((), (), s32[]{:S(2)}) async-start(), calls=%async_computation.12 | async-start | bytes 5898240 | tf_op jit(solution)/shard_map/reduce_scatter | solution.py:114
  390.0 11.9 %copy-start.13 = (bf16[2,1024,1024]{2,1,0:T(8,128)(2,1)S(1)}, bf16[2,1024,1024]{2,1,0:T(8,128)(2,1)}, u32[]{:S(2)}) copy-start(bf16[2,1024,1024]{2,1,0:T(8,128)(2,1)} %param.17) | copy-start | bytes 12582916
  402.0 3.5 copy-start.16
  410.4 189.1 %reduce-scatter.20.cloned.1.call-start = ((), (), s32[]{:S(2)}) async-start(), calls=%async_computation.15 | async-start | bytes 655360
  411.8 41.3 %copy-start.3 = (f32[256,1024]{1,0:T(8,128)S(1)}, f32[256,1024]{1,0:T(8,128)}, u32[]{:S(2)}) copy-start(f32[256,1024]{1,0:T(8,128)} %get-tuple-element.34) | copy-start | bytes 3145732
  501.7 120.5 %reduce-scatter.16.cloned.1.call-start = ((), (), s32[]{:S(2)}) async-start(), calls=%async_computation.13 | async-start | bytes 655360
  575.1 3.0 copy-start.2
  580.0 66.0 %all-to-all-start.3 = ((bf16[1,8,2,18,1024]{4,2,3,0,1:T(2,128)(2,1)}), bf16[1,8,2,18,1024]{4,2,3,0,1:T(2,128)(2,1)S(1)}, u32[]{:S(2)}, u32[]{:S(2)}) async-start(bf16[1,8,2,18,1024]{4,2,3,0,1:T(2,128)(2,1)} %copy.98), calls=%async_computation.5 | async-start | bytes 1179648 | tf_op jit(solution)/shard_map/all_to_all | solution.py:16
  583.6 60.8 %reduce-scatter.18.cloned.1.call-start = ((), (), s32[]{:S(2)}) async-start(), calls=%async_computation.14 | async-start | bytes 655360
  594.9 51.5 %copy-start.4 = (f32[256,1024]{1,0:T(8,128)S(1)}, f32[256,1024]{1,0:T(8,128)}, u32[]{:S(2)}) copy-start(f32[256,1024]{1,0:T(8,128)} %convert_add_fusion) | copy-start | bytes 3145732
Sparse Core Ops, SparseCore 0:
  20.5 53.1 all-gather.3
  132.7 82.3 reduce-scatter.11
  304.1 46.8 all-gather.5
  367.0 119.1 all-reduce.3
  489.0 86.0 reduce-scatter.13
  577.2 22.1 reduce-scatter.19
  602.3 19.8 reduce-scatter.15
  624.5 19.8 reduce-scatter.17
where the time goes:
time: 661 us; the launch traced here: 655 us
  waiting for transfers between devices  355 us (54%)
  blocking collectives  143 us (22%)
  matrix products  54.9 us (8%)
  local copies, waits for them, and re-layouts  47.1 us (7%)
  other arithmetic  23.5 us (4%)
  starting transfers between devices  16.7 us (3%)
  between operations  14.7 us (2%)
    all_gather x2, waiting for transfers between devices, spread_rows(): shared = lax.all_gather(buffer, 'hidden', axis=0, tiled=True)  100 us
    unnamed x12, waiting for transfers between devices  78.7 us
    reduce_scatter x1, waiting for transfers between devices, on_device(): lax.psum_scatter(jnp.einsum('hgjcf,jdf->hgjcd', piece, w_in, preferred_el...  73.4 us
    reduce_scatter x1, waiting for transfers between devices, on_device(): lax.psum_scatter(jnp.einsum('hgjcf,jfd->hgjcd', piece, w_out, preferred_e...  69.8 us
    all_gather x1, blocking collectives, on_device(): lax.all_gather(centroids.reshape(-1), ('expert', 'hidden'), axis=0, tiled...  68.8 us
    psum x1, blocking collectives, on_device(): lax.psum((jnp.sum(hot * gate[:, None], axis=0), jnp.sum(hot, axis=0)), ('...  38.2 us
    all_to_all x2, waiting for transfers between devices, spread_rows(): lax.all_to_all(shared, 'expert', split_axis=1, concat_axis=1, tiled=True)  32.7 us
  transfers between devices with their start and end apart: 12, of which 10 were waited for; matrix products, arithmetic and copies ran while one was open for 10% of the time, Pallas kernels for 0%

commit v1 on v0

v1 whole, which is shorter than its diff:
```python
import functools

import jax
import jax.numpy as jnp
from jax import lax
from jax.experimental import pallas as pl
from jax.experimental.pallas import tpu as pltpu
from jax.sharding import PartitionSpec as P

EPS = 1e-05
MESH = pl.DeviceIdType.MESH
F32 = jnp.float32
BF16 = jnp.bfloat16
TILE = 256
HALVES = 2
GELU_A = 0.7978845608028654
GELU_B = 0.044715


def contract(a, b, dims):
    return lax.dot_general(a, b, (dims, ((), ())), preferred_element_type=F32)


def iota(shape, axis):
    return lax.broadcasted_iota(jnp.int32, shape, axis)


def exchange_kernel(
    dims,
    tok, cot, asg, lens, cent, gain, bias, bout, bin_, win, wout,
    o_gat, o_act, o_pg, o_ret, o_slot, o_small, o_bg, o_mean,
    vwin, vwout, gat, act, pg, sbuf, rbuf, snd, rcv, rsnd, xg, pick, par, stats, zs, mg, grads, gbuf, fin,
    w_sem, par_s, par_r, zs_s, zs_r, mg_s, mg_r, gb_s, gb_r,
    disp_s, disp_r, ret_s, ret_r, gat_s, gat_r, red_s, red_r, out_sem,
):
    G, H, J, S, MSG, R, T, D, F, PW, seq_len = dims
    e, z = lax.axis_index("expert"), lax.axis_index("hidden")
    dtiles, ftiles = D // TILE, F // TILE
    DH = D // HALVES

    def cols(t, size=TILE):
        return pl.ds(pl.multiple_of(t * size, size), size)

    load_in = pltpu.make_async_copy(win, vwin, w_sem.at[0])
    load_out = pltpu.make_async_copy(wout, vwout, w_sem.at[1])
    load_in.start()
    load_out.start()

    barrier = pltpu.get_barrier_semaphore()
    for d in range(1, H):
        pl.semaphore_signal(barrier, inc=1, device_id=(e, (z + d) % H), device_id_type=MESH)
    for d in range(1, G):
        pl.semaphore_signal(barrier, inc=1, device_id=((e + d) % G, z), device_id_type=MESH)

    own_cols = cols(z, PW)
    par[pl.ds(0, J), own_cols] = gain[...]
    par[pl.ds(J, J), own_cols] = bias[...]
    par[pl.ds(2 * J, J), own_cols] = cent[...].astype(F32)
    par[pl.ds(3 * J, J), own_cols] = bout[...]

    expert = asg[...]
    place = (e * H + z) * T
    length = lens[place // seq_len]
    live = (place % seq_len + iota((T, 1), 0)) < length
    lane = iota((T, 128), 1)
    hot = ((expert == lane) & live).astype(F32)
    hot16 = hot.astype(BF16)
    earlier = (iota((T, T), 1) < iota((T, T), 0)).astype(F32).astype(BF16)
    before = contract(earlier, hot16, ((1,), (0,)))
    row_e = iota((1, 128), 1)
    group = lax.div(row_e, jnp.int32(J))
    inner = row_e - group * J
    base = (inner * (G * MSG) + group * MSG).astype(F32)
    slot = jnp.sum(hot * (before + base), axis=1, keepdims=True)
    slot = jnp.where(live, slot, -1.0)
    count_at = jnp.where(live, jnp.sum(hot * (base + 2.0 * S), axis=1, keepdims=True), -1.0)
    o_slot[...] = jnp.broadcast_to(slot, (T, 128))
    slot_i = slot.astype(jnp.int32)
    count_i = count_at.astype(jnp.int32)

    r = iota((R, G * MSG), 0)
    rk = jnp.floor((r.astype(F32) + 0.5) * (1.0 / S)).astype(jnp.int32)
    at = r + rk * (MSG - S)
    c = iota((R, G * MSG), 1)
    pick[pl.ds(0, R), :] = (c == at).astype(F32).astype(BF16)
    pick[pl.ds(R, R), :] = (c == at + S).astype(F32).astype(BF16)

    pl.semaphore_wait(barrier, (H - 1) + (G - 1))

    def par_copy(d, source):
        return pltpu.make_async_remote_copy(
            src_ref=par.at[:, cols(source, PW)], dst_ref=par.at[:, cols(source, PW)],
            send_sem=par_s.at[d], recv_sem=par_r.at[d],
            device_id=(e, (z + d) % H), device_id_type=MESH)

    for d in range(1, H):
        par_copy(d, z).start()

    def msg(k):
        return pl.ds(pl.multiple_of(k * MSG, MSG), MSG)

    def disp_copy(j, d, target):
        return pltpu.make_async_remote_copy(
            src_ref=snd.at[j, msg(target)], dst_ref=rcv.at[j, msg(e)],
            send_sem=disp_s.at[j, d], recv_sem=disp_r.at[j, d],
            device_id=(target, z), device_id_type=MESH)

    def disp_in(j, d):
        k = (e - d + G) % G
        return pltpu.make_async_remote_copy(
            src_ref=snd.at[j, msg(k)], dst_ref=rcv.at[j, msg(k)],
            send_sem=disp_s.at[j, d], recv_sem=disp_r.at[j, d],
            device_id=((e + d) % G, z), device_id_type=MESH)

    for j in range(J):
        m = iota((T, G * MSG), 1) + j * (G * MSG)
        to_tok = (slot_i == m).astype(F32).astype(BF16)
        to_cot = ((slot_i + S == m) & (slot_i >= 0)).astype(F32).astype(BF16)
        to_count = (count_i == m).astype(F32).astype(BF16)

        def fill(t, _, j=j, to_tok=to_tok, to_cot=to_cot):
            v = contract(to_tok, tok[:, cols(t)], ((0,), (0,)))
            v = v + contract(to_cot, cot[:, cols(t)], ((0,), (0,)))
            snd[j, :, cols(t)] = v.astype(BF16)
            return 0

        lax.fori_loop(0, dtiles, fill, 0)
        counts = contract(to_count, jnp.ones((T, 128), BF16), ((0,), (0,)))
        snd[j, :, pl.ds(0, 128)] = (snd[j, :, pl.ds(0, 128)].astype(F32) + counts).astype(BF16)
        for d in range(1, G):
            disp_copy(j, d, (e + d) % G).start()
        rcv[j, msg(e), :] = snd[j, msg(e), :]

    for d in range(1, H):
        par_copy(d, (z - d + H) % H).wait_recv()

    def gat_copy(a, j, chunk, up):
        return pltpu.make_async_remote_copy(
            src_ref=gat.at[a, j, chunk], dst_ref=gat.at[a, j, chunk],
            send_sem=gat_s.at[up, a, j, chunk], recv_sem=gat_r.at[a, j, chunk],
            device_id=(e, jnp.clip(z + 2 * up - 1, 0, H - 1)), device_id_type=MESH)

    def send_gat(a, j, chunk, up):
        @pl.when(jnp.where(up == 1, z < H - 1, z > 0))
        def _():
            gat_copy(a, j, chunk, up).start()

    def red_copy(a, j, half, home, up):
        slot_to = jnp.where(jnp.logical_and(up == 1, home == z + 1), H, home)
        return pltpu.make_async_remote_copy(
            src_ref=sbuf.at[a, j, home, :, pl.ds(half * DH, DH)],
            dst_ref=rbuf.at[a, j, slot_to, :, pl.ds(half * DH, DH)],
            send_sem=red_s.at[a, j, half, home], recv_sem=red_r.at[a, j, half, slot_to],
            device_id=(e, jnp.clip(z + 2 * up - 1, 0, H - 1)), device_id_type=MESH)

    def red_in(a, j, half, slot_at):
        return pltpu.make_async_remote_copy(
            src_ref=sbuf.at[a, j, 0, :, pl.ds(half * DH, DH)],
            dst_ref=rbuf.at[a, j, slot_at, :, pl.ds(half * DH, DH)],
            send_sem=red_s.at[a, j, half, 0], recv_sem=red_r.at[a, j, half, slot_at],
            device_id=(e, jnp.clip(z + 1, 0, H - 1)), device_id_type=MESH)

    gate_sums = jnp.zeros((8, 128), F32)
    live_counts = jnp.zeros((8, 128), F32)
    lane8 = iota((8, 128), 1)
    for j in range(J):
        for d in range(1, G):
            disp_in(j, d).wait_recv()

        def unpack(t, _, j=j):
            xg[j, :, cols(t)] = contract(pick[...], rcv[j, :, cols(t)], ((1,), (0,))).astype(BF16)
            return 0

        lax.fori_loop(0, dtiles, unpack, 0)
        rr = iota((R, G * MSG), 0)
        rrk = jnp.floor((rr.astype(F32) + 0.5) * (1.0 / S)).astype(jnp.int32)
        pick_count = (iota((R, G * MSG), 1) == rrk * MSG + 2 * S).astype(F32).astype(BF16)
        count = contract(pick_count, rcv[j, :, pl.ds(0, 128)], ((1,), (0,)))[:, 0:1]
        r1 = iota((R, 1), 0).astype(F32)
        rank = r1 - S * jnp.floor((r1 + 0.5) * (1.0 / S))
        filled = rank < count

        x = xg[j, pl.ds(0, R), :].astype(F32)
        score = jnp.sum(x * par[pl.ds(2 * J + j, 1), :], axis=1, keepdims=True)
        gate = jax.nn.sigmoid(score)
        mean = jnp.mean(x, axis=1, keepdims=True)
        centered = x - mean
        var = jnp.mean(centered * centered, axis=1, keepdims=True)
        factor = lax.rsqrt(var + EPS)
        lifted = centered * factor * par[pl.ds(j, 1), :] + par[pl.ds(J + j, 1), :]
        gat[0, j, z] = lifted.astype(BF16)
        send_gat(0, j, z, 1)
        send_gat(0, j, z, 0)
        gat[1, j, z] = (gate * xg[j, pl.ds(R, R), :].astype(F32)).astype(BF16)
        send_gat(1, j, z, 1)
        send_gat(1, j, z, 0)
        stats[0, j] = gate
        stats[1, j] = mean
        stats[2, j] = factor
        kept = jnp.where(filled, gate, 0.0)
        total = jnp.sum(kept, axis=0, keepdims=True)
        number = jnp.sum(filled.astype(F32), axis=0, keepdims=True)
        gate_sums = gate_sums + jnp.where(lane8 == j, total, 0.0)
        live_counts = live_counts + jnp.where(lane8 == j, number, 0.0)

    zs[z, pl.ds(0, 8), :] = gate_sums
    zs[z, pl.ds(8, 8), :] = live_counts

    def zs_copy(d, source):
        return pltpu.make_async_remote_copy(
            src_ref=zs.at[source], dst_ref=zs.at[source],
            send_sem=zs_s.at[d], recv_sem=zs_r.at[d],
            device_id=(e, (z + d) % H), device_id_type=MESH)

    for d in range(1, H):
        zs_copy(d, z).start()

    load_in.wait()
    load_out.wait()
    o_bg[...] = jnp.zeros_like(o_bg)

    def compute(chunk, j):
        def first(t, _):
            lifted = gat[0, j, chunk]
            pre = contract(lifted, vwin[j, :, cols(t)], ((1,), (0,))) + bin_[pl.ds(j, 1), cols(t)]
            sq = pre * pre
            th = jnp.tanh(pre * (GELU_A + (GELU_A * GELU_B) * sq))
            cdf = 0.5 + 0.5 * th
            slope = cdf + pre * (0.5 - 0.5 * th * th) * (GELU_A + (3.0 * GELU_A * GELU_B) * sq)
            act[j, chunk, :, cols(t)] = (pre * cdf).astype(BF16)
            act_grad = contract(gat[1, j, chunk], vwout[j, cols(t), :], ((1,), (1,)))
            pre_grad = (act_grad * slope).astype(BF16)
            pg[j, chunk, :, cols(t)] = pre_grad
            o_bg[pl.ds(j, 1), cols(t)] += jnp.sum(pre_grad.astype(F32), axis=0, keepdims=True)
            return 0

        lax.fori_loop(0, ftiles, first, 0)

        def second(t, _):
            v = contract(act[j, chunk], vwout[j, :, cols(t)], ((1,), (0,)))
            sbuf[0, j, chunk, :, cols(t)] = v.astype(BF16)
            w = contract(pg[j, chunk], vwin[j, cols(t), :], ((1,), (1,)))
            sbuf[1, j, chunk, :, cols(t)] = w.astype(BF16)
            return 0

        lax.fori_loop(0, dtiles, second, 0)

    def item(q, _):
        s, j = q // J, q % J
        for up in (1, 0):
            chunk = z - s if up else z + s
            there = (chunk >= 0) if up else (chunk < H)

            @pl.when(jnp.logical_and(s > 0, there))
            def _(chunk=chunk, up=up):
                for a in range(2):
                    gat_copy(a, j, chunk, up).wait_recv()
                    send_gat(a, j, chunk, up)

        def side(d, _):
            chunk = jnp.where(d == 0, z - s, z + s)
            there = jnp.logical_and(jnp.logical_and(chunk >= 0, chunk < H), jnp.logical_or(s > 0, d == 0))

            @pl.when(there)
            def _():
                compute(jnp.clip(chunk, 0, H - 1), j)

                @pl.when(jnp.logical_and(s > 0, jnp.where(d == 0, z == H - 1, z == 0)))
                def _():
                    for a in range(2):
                        for half in range(HALVES):
                            red_copy(a, j, half, jnp.clip(chunk, 0, H - 1), d).start()

            return 0

        lax.fori_loop(0, 2, side, 0)

        @pl.when(s > 0)
        def _():
            for a in range(2):
                for half in range(HALVES):
                    for k in range(2):
                        up = (k + jnp.where(z >= H // 2, 0, 1)) % 2
                        home = jnp.where(up == 1, s, H - 1 - s)
                        passes = jnp.where(up == 1, jnp.logical_and(z > 0, z < home), jnp.logical_and(z < H - 1, z > home))

                        @pl.when(passes)
                        def _(a=a, half=half, up=up, home=home):
                            red_in(a, j, half, home).wait_recv()
                            at = (a, j, home, slice(None), pl.ds(half * DH, DH))
                            sbuf[at] = (sbuf[at].astype(F32) + rbuf[at].astype(F32)).astype(BF16)
                            red_copy(a, j, half, home, up).start()

        return 0

    lax.fori_loop(0, J, item, 0)

    for d in range(1, H):
        zs_copy(d, (z - d + H) % H).wait_recv()
    both = zs[0]
    for h in range(1, H):
        both = both + zs[h]
    mg[e] = both[0:8] / jnp.maximum(both[8:16], 1.0)

    def mg_copy(d, source):
        return pltpu.make_async_remote_copy(
            src_ref=mg.at[source], dst_ref=mg.at[source],
            send_sem=mg_s.at[d], recv_sem=mg_r.at[d],
            device_id=((e + d) % G, z), device_id_type=MESH)

    for d in range(1, G):
        mg_copy(d, e).start()

    lax.fori_loop(J, H * J, item, 0)

    outs = [
        pltpu.make_async_copy(gat, o_gat, out_sem.at[0]),
        pltpu.make_async_copy(act, o_act, out_sem.at[1]),
        pltpu.make_async_copy(pg, o_pg, out_sem.at[2]),
    ]
    for copy in outs:
        copy.start()

    def ret_copy(j, d, target):
        return pltpu.make_async_remote_copy(
            src_ref=rsnd.at[j, msg(target)], dst_ref=o_ret.at[j, msg(e)],
            send_sem=ret_s.at[j, d], recv_sem=ret_r.at[j, d],
            device_id=(target, z), device_id_type=MESH)

    def ret_in(j, d):
        k = (e - d + G) % G
        return pltpu.make_async_remote_copy(
            src_ref=rsnd.at[j, msg(k)], dst_ref=o_ret.at[j, msg(k)],
            send_sem=ret_s.at[j, d], recv_sem=ret_r.at[j, d],
            device_id=((e + d) % G, z), device_id_type=MESH)

    def ret_own(j):
        return pltpu.make_async_copy(rsnd.at[j, msg(e)], o_ret.at[j, msg(e)], out_sem.at[3 + j])

    for j in range(J):
        for half in range(HALVES):
            for a in range(2):
                at = (a, j, z, slice(None), pl.ds(half * DH, DH))
                low = (a, j, H, slice(None), pl.ds(half * DH, DH))
                to = (a, slice(None), pl.ds(half * DH, DH))
                fin[to] = sbuf[at].astype(F32)

                @pl.when(z < H - 1)
                def _(a=a, half=half, at=at, to=to):
                    red_in(a, j, half, z).wait_recv()
                    fin[to] += rbuf[at].astype(F32)

                @pl.when(z > 0)
                def _(a=a, half=half, low=low, to=to):
                    red_in(a, j, half, H).wait_recv()
                    fin[to] += rbuf[low].astype(F32)

        gate, mean, factor = stats[0, j], stats[1, j], stats[2, j]
        x = xg[j, pl.ds(0, R), :].astype(F32)
        g = xg[j, pl.ds(R, R), :].astype(F32)
        branch = (fin[0] + par[pl.ds(3 * J + j, 1), :]).astype(BF16).astype(F32)
        score_grad = jnp.sum(g * branch, axis=1, keepdims=True) * gate * (1.0 - gate)
        grads[pl.ds(2 * J + j, 1), :] = jnp.sum(score_grad * x, axis=0, keepdims=True)
        grads[pl.ds(3 * J + j, 1), :] = jnp.sum(gat[1, j, z].astype(F32), axis=0, keepdims=True)
        mixed = (x + gate * branch).astype(BF16)
        lifted_grad = fin[1]
        normed = (x - mean) * factor
        grads[pl.ds(j, 1), :] = jnp.sum(lifted_grad * normed, axis=0, keepdims=True)
        grads[pl.ds(J + j, 1), :] = jnp.sum(lifted_grad, axis=0, keepdims=True)
        n_grad = lifted_grad * par[pl.ds(j, 1), :]
        rows_grad = factor * (
            n_grad
            - jnp.mean(n_grad, axis=1, keepdims=True)
            - normed * jnp.mean(n_grad * normed, axis=1, keepdims=True)
        )
        rows_grad = rows_grad.astype(BF16).astype(F32)
        xg[j, pl.ds(0, R), :] = mixed
        xg[j, pl.ds(R, R), :] = (g + score_grad * par[pl.ds(2 * J + j, 1), :] + rows_grad).astype(BF16)

        def repack(t, _, j=j):
            rsnd[j, :, cols(t)] = contract(pick[...], xg[j, :, cols(t)], ((0,), (0,))).astype(BF16)
            return 0

        lax.fori_loop(0, dtiles, repack, 0)
        for d in range(1, G):
            ret_copy(j, d, (e + d) % G).start()
        ret_own(j).start()

    def gb_copy(d, source, target):
        return pltpu.make_async_remote_copy(
            src_ref=grads.at[:, cols(target, PW)], dst_ref=gbuf.at[source],
            send_sem=gb_s.at[d], recv_sem=gb_r.at[d],
            device_id=(e, (z + d) % H), device_id_type=MESH)

    for d in range(1, H):
        gb_copy(d, z, (z + d) % H).start()
    gbuf[z] = grads[:, own_cols]

    for d in range(1, G):
        mg_copy(d, (e - d + G) % G).wait_recv()
    means = jnp.zeros((8, 128), F32)
    for k in range(G):
        v = mg[k] if k == 0 else pltpu.roll(mg[k], k * J, 1)
        means = jnp.where((lane8 >= k * J) & (lane8 < k * J + J), v, means)
    o_mean[...] = means

    for d in range(1, H):
        gb_copy(d, (z - d + H) % H, z).wait_recv()
    small = gbuf[0]
    for h in range(1, H):
        small = small + gbuf[h]
    o_small[...] = small

    for j in range(J):
        for d in range(1, G):
            ret_in(j, d).wait_recv()
        ret_own(j).wait()
    for copy in outs:
        copy.wait()

    for d in range(1, H):
        par_copy(d, z).wait_send()
        zs_copy(d, z).wait_send()
        gb_copy(d, z, (z + d) % H).wait_send()
    for d in range(1, G):
        mg_copy(d, e).wait_send()
        for j in range(J):
            disp_copy(j, d, (e + d) % G).wait_send()
            ret_copy(j, d, (e + d) % G).wait_send()
    for a in range(2):
        for j in range(J):
            for h in range(H):

                @pl.when(jnp.logical_and(z < H - 1, h <= z))
                def _(a=a, j=j, h=h):
                    gat_copy(a, j, h, 1).wait_send()

                @pl.when(jnp.logical_and(z > 0, h >= z))
                def _(a=a, j=j, h=h):
                    gat_copy(a, j, h, 0).wait_send()

                @pl.when(h != z)
                def _(a=a, j=j, h=h):
                    for half in range(HALVES):
                        red_copy(a, j, half, h, jnp.where(h > z, 1, 0)).wait_send()


def local_kernel(
    dims,
    lift, pg, act, grad, ret, slot, tok, cot, small, bg, mean,
    o_mixed, o_tg, o_cent, o_gain, o_bias, o_win, o_bin, o_wout, o_bout, o_mean,
):
    G, H, J, S, MSG, R, T, D, F, PW, seq_len = dims
    o_win[0] = contract(lift[0, 0], pg[0], ((0,), (0,)))
    o_wout[0] = contract(act[0], grad[0, 0], ((0,), (0,)))

    first = jnp.logical_and(pl.program_id(0) == 0, pl.program_id(1) == 0)

    @pl.when(first)
    def _():
        o_gain[...] = small[pl.ds(0, J), :]
        o_bias[...] = small[pl.ds(J, J), :]
        o_cent[...] = small[pl.ds(2 * J, J), :]
        o_bout[...] = small[pl.ds(3 * J, J), :]
        o_bin[...] = bg[...]
        o_mean[...] = mean[pl.ds(0, 1), pl.ds(0, G * J)]
        spot = slot[:, 0:1].astype(jnp.int32)
        n = J * G * MSG
        m = iota((T, n), 1)
        live = spot >= 0
        to_mixed = (spot == m).astype(F32).astype(BF16)
        to_grad = ((spot + S == m) & live).astype(F32).astype(BF16)

        def place(t, _):
            at = pl.ds(pl.multiple_of(t * TILE, TILE), TILE)
            v = contract(to_mixed, ret[:, at], ((1,), (0,)))
            o_mixed[:, at] = jnp.where(live, v, tok[:, at].astype(F32)).astype(BF16)
            w = contract(to_grad, ret[:, at], ((1,), (0,)))
            o_tg[:, at] = jnp.where(live, w, cot[:, at].astype(F32)).astype(BF16)
            return 0

        lax.fori_loop(0, D // TILE, place, 0)


def on_device(
    tokens, assignment, lengths, centroids, ln_gain, ln_bias, w_in, b_in, w_out, b_out, cotangent
):
    T, D = tokens.shape
    G, H = lax.axis_size("expert"), lax.axis_size("hidden")
    J, F = w_in.shape[0], w_in.shape[2]
    PW = centroids.shape[1]
    S = max(2, 9 * T // (8 * J * G))
    MSG = -(-(2 * S + 1) // 16) * 16
    R = G * S
    seq_len = min(2048, H * T)
    dims = (G, H, J, S, MSG, R, T, D, F, PW, seq_len)
    vm = pl.BlockSpec(memory_space=pltpu.VMEM)
    hbm = pl.BlockSpec(memory_space=pl.ANY)
    sm = pl.BlockSpec(memory_space=pltpu.SMEM)
    dma = pltpu.SemaphoreType.DMA
    shape = jax.ShapeDtypeStruct
    gat, act, pg, ret, slot, small, bg, mean = pl.pallas_call(
        functools.partial(exchange_kernel, dims),
        name="exchange",
        out_shape=[
            shape((2, J, H, R, D), BF16),
            shape((J, H, R, F), BF16),
            shape((J, H, R, F), BF16),
            shape((J, G * MSG, D), BF16),
            shape((T, 128), F32),
            shape((4 * J, PW), F32),
            shape((J, F), F32),
            shape((8, 128), F32),
        ],
        in_specs=[vm, vm, vm, sm, vm, vm, vm, vm, vm, hbm, hbm],
        out_specs=[hbm, hbm, hbm, hbm, vm, vm, vm, vm],
        scratch_shapes=[
            pltpu.VMEM((J, D, F), BF16),
            pltpu.VMEM((J, F, D), BF16),
            pltpu.VMEM((2, J, H, R, D), BF16),
            pltpu.VMEM((J, H, R, F), BF16),
            pltpu.VMEM((J, H, R, F), BF16),
            pltpu.VMEM((2, J, H, R, D), BF16),
            pltpu.VMEM((2, J, H + 1, R, D), BF16),
            pltpu.VMEM((J, G * MSG, D), BF16),
            pltpu.VMEM((J, G * MSG, D), BF16),
            pltpu.VMEM((J, G * MSG, D), BF16),
            pltpu.VMEM((J, 2 * R, D), BF16),
            pltpu.VMEM((2 * R, G * MSG), BF16),
            pltpu.VMEM((4 * J, D), F32),
            pltpu.VMEM((3, J, R, 1), F32),
            pltpu.VMEM((H, 16, 128), F32),
            pltpu.VMEM((G, 8, 128), F32),
            pltpu.VMEM((4 * J, D), F32),
            pltpu.VMEM((H, 4 * J, PW), F32),
            pltpu.VMEM((2, R, D), F32),
            dma((2,)),
            dma((H,)), dma((H,)),
            dma((H,)), dma((H,)),
            dma((G,)), dma((G,)),
            dma((H,)), dma((H,)),
            dma((J, G)), dma((J, G)),
            dma((J, G)), dma((J, G)),
            dma((2, 2, J, H)), dma((2, J, H)),
            dma((2, J, HALVES, H)), dma((2, J, HALVES, H + 1)),
            dma((3 + J,)),
        ],
        compiler_params=pltpu.CompilerParams(
            collective_id=0, has_side_effects=True, vmem_limit_bytes=56 * 2**20
        ),
        cost_estimate=pl.CostEstimate(
            flops=16 * J * H * R * D * F // 2, bytes_accessed=30 * 2**20, transcendentals=J * H * R * F
        ),
    )(tokens, cotangent, assignment, lengths, centroids, ln_gain, ln_bias, b_out, b_in, w_in, w_out)

    N = H * R
    both = gat.reshape(2, J, N, D)
    full = lambda *shape: pl.BlockSpec(shape, lambda j, t: (0,) * len(shape))
    outs = pl.pallas_call(
        functools.partial(local_kernel, dims),
        name="gradients",
        grid=(J, F // TILE),
        out_shape=[
            shape((T, D), BF16),
            shape((T, D), BF16),
            shape((J, PW), F32),
            shape((J, PW), F32),
            shape((J, PW), F32),
            shape((J, D, F), F32),
            shape((J, F), F32),
            shape((J, F, D), F32),
            shape((J, PW), F32),
            shape((1, G * J), F32),
        ],
        in_specs=[
            pl.BlockSpec((1, 1, N, D), lambda j, t: (0, j, 0, 0)),
            pl.BlockSpec((1, N, TILE), lambda j, t: (j, 0, t)),
            pl.BlockSpec((1, N, TILE), lambda j, t: (j, 0, t)),
            pl.BlockSpec((1, 1, N, D), lambda j, t: (1, j, 0, 0)),
            full(J * G * MSG, D),
            full(T, 128),
            full(T, D),
            full(T, D),
            full(4 * J, PW),
            full(J, F),
            full(8, 128),
        ],
        out_specs=[
            full(T, D),
            full(T, D),
            full(J, PW),
            full(J, PW),
            full(J, PW),
            pl.BlockSpec((1, D, TILE), lambda j, t: (j, 0, t)),
            full(J, F),
            pl.BlockSpec((1, TILE, D), lambda j, t: (j, t, 0)),
            full(J, PW),
            full(1, G * J),
        ],
        compiler_params=pltpu.CompilerParams(
            dimension_semantics=("arbitrary", "arbitrary"), vmem_limit_bytes=48 * 2**20
        ),
        cost_estimate=pl.CostEstimate(
            flops=4 * J * N * D * F, bytes_accessed=28 * 2**20, transcendentals=0
        ),
    )(both, pg.reshape(J, N, F), act.reshape(J, N, F), both, ret.reshape(J * G * MSG, D), slot, tokens, cotangent, small, bg, mean)
    return (*outs[:9], outs[9].reshape(G * J))


def solution(mesh):
    tok = P(("expert", "hidden"), None)
    par = P("expert", "hidden")
    win = P("expert", None, "hidden")
    wout = P("expert", "hidden", None)
    return jax.shard_map(
        on_device,
        mesh=mesh,
        in_specs=(tok, tok, P(), par, par, par, win, par, wout, par, tok),
        out_specs=(tok, tok, par, par, par, win, par, wout, par, P()),
        check_vma=False,
    )
```

time: 661 us -> 190 us (0.29)
  the two profiles are of different devices: /device:TPU:0 before, /device:TPU:11 now
where the time goes in v1:
time: 190 us; the launch traced here: 189 us
  Pallas kernels  181 us (95%)
  local copies, waits for them, and re-layouts  7.52 us (4%)
    pallas_call x1, Pallas kernels, on_device(): pl.pallas_call(functools.partial(exchange_kernel, dims), name='exchange',...  165 us
    pallas_call x1, Pallas kernels, on_device(): pl.pallas_call(functools.partial(local_kernel, dims), name='gradients', g...  16.4 us
    unnamed x17, local copies, waits for them, and re-layouts  7.52 us

profile of v1, /device:TPU:11, one launch (start us, length us, event | category | flops | bytes accessed | tf_op | source)
XLA Modules:
  0.0 189.3 jit_solution(4603967183666162297)
XLA Ops:
  0.6 1.5 copy.21.asg
  2.1 0.0 copy-start
  2.1 0.0 copy-start.1
  2.1 164.7 %exchange.1 = (bf16[2,2,4,144,1024]{4,3,2,1,0:T(8,128)(2,1)}, bf16[2,4,144,1024]{3,2,1,0:T(8,128)(2,1)}, bf16[2,4,144,1024]{3,2,1,0:T(8,128)(2,1)}, bf16[2,384,1...) custom-call(bf16[256,1024]{1,0:T(8,128)(2,1)} %tok.3, ...), custom_call_target="tpu_custom_call" | custom-call | flops 9663676416 | bytes 31457280 | tf_op jit(solution)/shard_map/exchange/pallas_call | solution.py:502
  166.8 0.0 copy-done
  166.8 0.0 copy-done.1
  166.9 0.0 copy-start.2
  166.9 1.7 copy-done.2
  168.5 0.0 copy-start.3
  168.5 1.4 copy-done.3
  169.9 0.0 copy-start.4
  169.9 0.9 copy-done.4
  170.8 0.0 copy-start.5
  170.8 0.7 copy-done.5
  171.5 0.0 copy-start.6
  171.5 0.7 copy-done.6
  172.2 0.0 copy-start.7
  172.2 0.7 copy-done.7
  172.9 16.4 %gradients.1 = (bf16[256,1024]{1,0:T(8,128)(2,1)}, bf16[256,1024]{1,0:T(8,128)(2,1)}, f32[2,256]{1,0:T(2,128)}, f32[2,256]{1,0:T(2,128)}, f32[2,256]{1,0:T(2,128...) custom-call(bf16[2,2,576,1024]{3,2,1,0:T(8,128)(2,1)} %bitcast.7, ...), custom_call_target="tpu_custom_call" | custom-call | flops 4831838208 | bytes 29360128 | tf_op jit(solution)/shard_map/gradients/pallas_call | solution.py:559
Async XLA Ops:
  2.1 164.7 %copy-start = (bf16[256,1024]{1,0:T(8,128)(2,1)S(1)}, bf16[256,1024]{1,0:T(8,128)(2,1)}, u32[]{:S(2)}) copy-start(bf16[256,1024]{1,0:T(8,128)(2,1)} %tok.3) | copy-start | bytes 1572868
  2.1 164.7 %copy-start.1 = (bf16[256,1024]{1,0:T(8,128)(2,1)S(1)}, bf16[256,1024]{1,0:T(8,128)(2,1)}, u32[]{:S(2)}) copy-start(bf16[256,1024]{1,0:T(8,128)(2,1)} %cot.3) | copy-start | bytes 1572868
  166.9 1.7 copy-start.2
  168.5 1.4 copy-start.3
  169.9 0.9 copy-start.4
  170.8 0.7 copy-start.5
  171.5 0.7 copy-start.6
  172.2 0.7 copy-start.7

commit v2 on v1

v2 whole, which is shorter than its diff:
```python
import functools

import jax
import jax.numpy as jnp
from jax import lax
from jax.experimental import pallas as pl
from jax.experimental.pallas import tpu as pltpu
from jax.sharding import PartitionSpec as P

EPS = 1e-05
MESH = pl.DeviceIdType.MESH
F32 = jnp.float32
BF16 = jnp.bfloat16
TILE = 256
HALVES = 2
GELU_A = 0.7978845608028654
GELU_B = 0.044715
SHAPES = ((8, 8, 8, 8), (8, 7, 5, 4),)


def contract(a, b, dims=((1,), (0,))):
    return lax.dot_general(a, b, (dims, ((), ())), preferred_element_type=F32)


def iota(shape, axis):
    return lax.broadcasted_iota(jnp.int32, shape, axis)


def ones_where(mask):
    return mask.astype(F32).astype(BF16)


def per(index, size, count):
    return jnp.floor((index.astype(F32) + 0.5) * (1.0 / size)).astype(jnp.int32)


def exchange_kernel(
    dims, sizes,
    asg, lens, cent, gain, bias, bout, bin_, tok_in, cot_in, win, wout,
    o_gat, o_act, o_pg, o_ret, o_slot, o_small, o_bg, o_mean,
    tok, cot, vwin, vwout, gat, act, pg, sbuf, rbuf, snd, rcv, rsnd, xg, spread, pick, unpick, pick_count,
    par, stats, zs, mg, grads, gbuf, scores,
    w_sem, par_s, par_r, zs_s, zs_r, mg_s, mg_r, gb_s, gb_r,
    disp_s, disp_r, ret_s, ret_r, gat_s, gat_r, red_s, red_r, out_sem,
):
    G, H, J, S, MSG, R, T, D, F, PW, seq_len = dims
    e, z = lax.axis_index("expert"), lax.axis_index("hidden")
    E = G * J
    GM = G * MSG
    parts, ftiles = D // TILE, F // TILE
    DH = D // HALVES

    def cols(t, size=TILE):
        return pl.ds(pl.multiple_of(t * size, size), size)

    barrier = pltpu.get_barrier_semaphore()
    for d in range(1, H):
        pl.semaphore_signal(barrier, inc=1, device_id=(e, (z + d) % H), device_id_type=MESH)
    for d in range(1, G):
        pl.semaphore_signal(barrier, inc=1, device_id=((e + d) % G, z), device_id_type=MESH)

    loads = [
        pltpu.make_async_copy(a, b, w_sem.at[i])
        for i, (a, b) in enumerate(((tok_in, tok), (cot_in, cot), (win, vwin), (wout, vwout)))
    ]
    for copy in loads:
        copy.start()

    own_cols = cols(z, PW)
    par[pl.ds(0, J), own_cols] = gain[...]
    par[pl.ds(J, J), own_cols] = bias[...]
    par[pl.ds(2 * J, J), own_cols] = cent[...].astype(F32)
    par[pl.ds(3 * J, J), own_cols] = bout[...]

    expert = asg[...]
    place = (e * H + z) * T
    length = lens[place // seq_len]
    live = (place % seq_len + iota((1, T), 1)) < length
    sub_e = iota((E, 1), 0)
    hot = ((expert == sub_e) & live).astype(F32)
    earlier = ones_where(iota((T, T), 0) < iota((T, T), 1))
    before = contract(hot.astype(BF16), earlier)
    group = per(sub_e, J, G)
    inner = sub_e - group * J
    rank = jnp.sum(hot * before, axis=0, keepdims=True).astype(jnp.int32)
    to_group = jnp.sum(hot * group.astype(F32), axis=0, keepdims=True).astype(jnp.int32)
    to_inner = jnp.sum(hot * inner.astype(F32), axis=0, keepdims=True).astype(jnp.int32)
    to_inner = jnp.where(live, to_inner, -1)
    message = to_group * MSG
    o_slot[...] = jnp.broadcast_to(jnp.where(live, to_inner * GM + message + rank, -D * D), (8, T))

    pl.semaphore_wait(barrier, (H - 1) + (G - 1))

    def par_copy(d, source):
        return pltpu.make_async_remote_copy(
            src_ref=par.at[:, cols(source, PW)], dst_ref=par.at[:, cols(source, PW)],
            send_sem=par_s.at[d], recv_sem=par_r.at[d],
            device_id=(e, (z + d) % H), device_id_type=MESH)

    for d in range(1, H):
        par_copy(d, z).start()

    def msg(k):
        return pl.ds(pl.multiple_of(k * MSG, MSG), MSG)

    def disp_copy(j, a, d, target):
        return pltpu.make_async_remote_copy(
            src_ref=snd.at[j, a, msg(target)], dst_ref=rcv.at[j, a, msg(e)],
            send_sem=disp_s.at[j, a, d], recv_sem=disp_r.at[j, a, d],
            device_id=(target, z), device_id_type=MESH)

    def disp_in(j, a, d):
        k = (e - d + G) % G
        return pltpu.make_async_remote_copy(
            src_ref=snd.at[j, a, msg(k)], dst_ref=rcv.at[j, a, msg(k)],
            send_sem=disp_s.at[j, a, d], recv_sem=disp_r.at[j, a, d],
            device_id=((e + d) % G, z), device_id_type=MESH)

    for j in range(J):
        mine = to_inner == j
        at = jnp.where(mine, message + rank, -D * D)
        row = iota((GM, T), 0)
        for part in range(parts):
            spread[part] = ones_where(at + part * S == row)
        for a, source in enumerate((tok, cot)):
            if j == 0:
                loads[a].wait()
            v = contract(spread[0], source[:, pl.ds(0, TILE)])
            for part in range(1, parts):
                v = v + contract(spread[part], source[:, pl.ds(part * TILE, TILE)])
            if a == 0:
                to_count = ones_where(jnp.where(mine, message + parts * S, -1) == row)
                v = v + contract(to_count, jnp.ones((T, TILE), BF16))
            snd[j, a] = v.astype(BF16)
            for d in range(1, G):
                disp_copy(j, a, d, (e + d) % G).start()
            rcv[j, a, msg(e), :] = snd[j, a, msg(e), :]

    def row_of(c):
        k = per(c, MSG, G)
        start = jnp.full(c.shape, -D * D, jnp.int32)
        filled_before = jnp.int32(0)
        for i in range(G):
            first = (i * H + z) * T
            some = lens[first // seq_len] > first % seq_len
            start = jnp.where((k == i) & some, filled_before * S, start)
            filled_before = filled_before + some.astype(jnp.int32)
        return start, c - k * MSG

    start, within = row_of(iota((1, GM), 1))
    down = iota((R, GM), 0)
    for part in range(parts):
        i = within - part * S
        pick[part] = ones_where(jnp.where((i >= 0) & (i < S), start + i, -1) == down)
    counts_at = jnp.where(within == parts * S, start, -D * D)
    pick_count[...] = ones_where((down >= counts_at) & (down < counts_at + S))
    start, within = row_of(iota((GM, 1), 0))
    across = iota((GM, R), 1)
    for part in range(parts):
        i = within - part * S
        unpick[part] = ones_where(jnp.where((i >= 0) & (i < S), start + i, -1) == across)

    for h in range(H):
        if sizes[h] < R:
            gat[:, :, h, pl.ds(sizes[h], R - sizes[h]), :] = jnp.zeros((2, J, R - sizes[h], D), BF16)

    @pl.when(z == 0)
    def _():
        rbuf[:, :, H] = jnp.zeros((2, J, R, D), BF16)

    @pl.when(z == H - 1)
    def _():
        rbuf[:, :, H - 1] = jnp.zeros((2, J, R, D), BF16)

    o_bg[...] = jnp.zeros_like(o_bg)

    for d in range(1, H):
        par_copy(d, (z - d + H) % H).wait_recv()

    def with_rows(chunk, body):
        for size in sorted(set(sizes)):
            planes = [h for h in range(H) if sizes[h] == size]
            if len(planes) == H:
                body(size)
            else:
                hit = chunk == planes[0]
                for h in planes[1:]:
                    hit = jnp.logical_or(hit, chunk == h)
                pl.when(hit)(functools.partial(body, size))

    def gat_copy(a, j, chunk, up, size):
        return pltpu.make_async_remote_copy(
            src_ref=gat.at[a, j, chunk, pl.ds(0, size)], dst_ref=gat.at[a, j, chunk, pl.ds(0, size)],
            send_sem=gat_s.at[up, a, j, chunk], recv_sem=gat_r.at[a, j, chunk],
            device_id=(e, jnp.clip(z + 2 * up - 1, 0, H - 1)), device_id_type=MESH)

    def send_gat(a, j, chunk, up, size):
        @pl.when(jnp.where(up == 1, z < H - 1, z > 0))
        def _():
            gat_copy(a, j, chunk, up, size).start()

    def send_own(a, j):
        def both(size):
            send_gat(a, j, z, 1, size)
            send_gat(a, j, z, 0, size)

        with_rows(z, both)

    def red_copy(a, j, half, home, up, size):
        slot_to = jnp.where(jnp.logical_and(up == 1, home == z + 1), H, home)
        at = (pl.ds(0, size), pl.ds(half * DH, DH))
        return pltpu.make_async_remote_copy(
            src_ref=sbuf.at[(a, j, home, *at)], dst_ref=rbuf.at[(a, j, slot_to, *at)],
            send_sem=red_s.at[a, j, half, home], recv_sem=red_r.at[a, j, half, slot_to],
            device_id=(e, jnp.clip(z + 2 * up - 1, 0, H - 1)), device_id_type=MESH)

    def red_in(a, j, half, slot_at, size):
        at = (pl.ds(0, size), pl.ds(half * DH, DH))
        return pltpu.make_async_remote_copy(
            src_ref=sbuf.at[(a, j, 0, *at)], dst_ref=rbuf.at[(a, j, slot_at, *at)],
            send_sem=red_s.at[a, j, half, 0], recv_sem=red_r.at[a, j, half, slot_at],
            device_id=(e, jnp.clip(z + 1, 0, H - 1)), device_id_type=MESH)

    gate_sums = jnp.zeros((8, 128), F32)
    live_counts = jnp.zeros((8, 128), F32)
    lane8 = iota((8, 128), 1)
    r1 = iota((R, 1), 0)
    rank_in = r1 - S * per(r1, S, G)
    for j in range(J):
        for d in range(1, G):
            disp_in(j, 0, d).wait_recv()
        for part in range(parts):
            xg[j, 0, :, pl.ds(part * TILE, TILE)] = contract(pick[part], rcv[j, 0]).astype(BF16)
        count = contract(pick_count[...], rcv[j, 0, :, pl.ds(0, 128)])[:, 0:1]
        filled = rank_in.astype(F32) < count

        x = xg[j, 0].astype(F32)
        mean = jnp.mean(x, axis=1, keepdims=True)
        centered = x - mean
        var = jnp.mean(centered * centered, axis=1, keepdims=True)
        factor = lax.rsqrt(var + EPS)
        lifted = centered * factor * par[pl.ds(j, 1), :] + par[pl.ds(J + j, 1), :]
        gat[0, j, z] = lifted.astype(BF16)
        send_own(0, j)

        score = jnp.sum(x * par[pl.ds(2 * J + j, 1), :], axis=1, keepdims=True)
        gate = jax.nn.sigmoid(score)
        for d in range(1, G):
            disp_in(j, 1, d).wait_recv()
        for part in range(parts):
            at = pl.ds(part * TILE, TILE)
            g = contract(pick[part], rcv[j, 1])
            xg[j, 1, :, at] = g.astype(BF16)
            gat[1, j, z, :, at] = (gate * g).astype(BF16)
        send_own(1, j)
        stats[0, j] = gate
        stats[1, j] = mean
        stats[2, j] = factor
        stats[3, j] = filled.astype(F32)
        total = jnp.sum(jnp.where(filled, gate, 0.0), axis=0, keepdims=True)
        number = jnp.sum(filled.astype(F32), axis=0, keepdims=True)
        gate_sums = gate_sums + jnp.where(lane8 == j, total, 0.0)
        live_counts = live_counts + jnp.where(lane8 == j, number, 0.0)

    zs[z, pl.ds(0, 8), :] = gate_sums
    zs[z, pl.ds(8, 8), :] = live_counts

    def zs_copy(d, source):
        return pltpu.make_async_remote_copy(
            src_ref=zs.at[source], dst_ref=zs.at[source],
            send_sem=zs_s.at[d], recv_sem=zs_r.at[d],
            device_id=(e, (z + d) % H), device_id_type=MESH)

    for d in range(1, H):
        zs_copy(d, z).start()

    loads[2].wait()
    loads[3].wait()

    def compute(chunk, j):
        def first(t, _):
            pre = contract(gat[0, j, chunk], vwin[j, :, cols(t)]) + bin_[pl.ds(j, 1), cols(t)]
            sq = pre * pre
            th = jnp.tanh(pre * (GELU_A + (GELU_A * GELU_B) * sq))
            cdf = 0.5 + 0.5 * th
            slope = cdf + pre * (0.5 - 0.5 * th * th) * (GELU_A + (3.0 * GELU_A * GELU_B) * sq)
            act[j, chunk, :, cols(t)] = (pre * cdf).astype(BF16)
            act_grad = contract(gat[1, j, chunk], vwout[j, cols(t), :], ((1,), (1,)))
            pre_grad = (act_grad * slope).astype(BF16)
            pg[j, chunk, :, cols(t)] = pre_grad
            o_bg[pl.ds(j, 1), cols(t)] += jnp.sum(pre_grad.astype(F32), axis=0, keepdims=True)
            return 0

        lax.fori_loop(0, ftiles, first, 0)

        def second(t, _):
            v = contract(act[j, chunk], vwout[j, :, cols(t)])
            sbuf[0, j, chunk, :, cols(t)] = v.astype(BF16)
            w = contract(pg[j, chunk], vwin[j, cols(t), :], ((1,), (1,)))
            sbuf[1, j, chunk, :, cols(t)] = w.astype(BF16)
            return 0

        lax.fori_loop(0, parts, second, 0)

    def mg_copy(d, source):
        return pltpu.make_async_remote_copy(
            src_ref=mg.at[source], dst_ref=mg.at[source],
            send_sem=mg_s.at[d], recv_sem=mg_r.at[d],
            device_id=((e + d) % G, z), device_id_type=MESH)

    def gb_copy(d, source, target):
        return pltpu.make_async_remote_copy(
            src_ref=grads.at[:, cols(target, PW)], dst_ref=gbuf.at[source],
            send_sem=gb_s.at[d], recv_sem=gb_r.at[d],
            device_id=(e, (z + d) % H), device_id_type=MESH)

    outs = [
        pltpu.make_async_copy(gat, o_gat, out_sem.at[0]),
        pltpu.make_async_copy(act, o_act, out_sem.at[1]),
        pltpu.make_async_copy(pg, o_pg, out_sem.at[2]),
    ]

    def ret_copy(j, a, d, target):
        return pltpu.make_async_remote_copy(
            src_ref=rsnd.at[a, j, msg(target)], dst_ref=o_ret.at[a, j, msg(e)],
            send_sem=ret_s.at[j, a, d], recv_sem=ret_r.at[j, a, d],
            device_id=(target, z), device_id_type=MESH)

    def ret_in(j, a, d):
        k = (e - d + G) % G
        return pltpu.make_async_remote_copy(
            src_ref=rsnd.at[a, j, msg(k)], dst_ref=o_ret.at[a, j, msg(k)],
            send_sem=ret_s.at[j, a, d], recv_sem=ret_r.at[j, a, d],
            device_id=((e + d) % G, z), device_id_type=MESH)

    def ret_own(j, a):
        return pltpu.make_async_copy(rsnd.at[a, j, msg(e)], o_ret.at[a, j, msg(e)], out_sem.at[3 + 2 * j + a])

    def summed(a, j):
        for half in range(HALVES):
            @pl.when(z < H - 1)
            def _(half=half):
                with_rows(z, lambda size: red_in(a, j, half, z, size).wait_recv())

            @pl.when(z > 0)
            def _(half=half):
                with_rows(z, lambda size: red_in(a, j, half, H, size).wait_recv())

        v = sbuf[a, j, z].astype(F32) + rbuf[a, j, z].astype(F32) + rbuf[a, j, H].astype(F32)
        return jnp.where(stats[3, j] > 0.5, v, 0.0)

    def send_home(a, j):
        v = contract(unpick[0], xg[j, a, :, pl.ds(0, TILE)])
        for part in range(1, parts):
            v = v + contract(unpick[part], xg[j, a, :, pl.ds(part * TILE, TILE)])
        rsnd[a, j] = v.astype(BF16)
        for d in range(1, G):
            ret_copy(j, a, d, (e + d) % G).start()
        ret_own(j, a).start()

    def finish(j, _):
        gate, mean, factor = stats[0, j], stats[1, j], stats[2, j]
        branch = (summed(0, j) + par[pl.ds(3 * J + j, 1), :]).astype(BF16).astype(F32)
        x = xg[j, 0].astype(F32)
        score_grad = jnp.sum(xg[j, 1].astype(F32) * branch, axis=1, keepdims=True) * gate * (1.0 - gate)
        grads[pl.ds(2 * J + j, 1), :] = jnp.sum(score_grad * x, axis=0, keepdims=True)
        grads[pl.ds(3 * J + j, 1), :] = jnp.sum(gat[1, j, z].astype(F32), axis=0, keepdims=True)
        scores[j] = ((x - mean) * factor).astype(F32)
        xg[j, 0] = (x + gate * branch).astype(BF16)
        send_home(0, j)
        lifted_grad = summed(1, j)
        normed = scores[j]
        grads[pl.ds(j, 1), :] = jnp.sum(lifted_grad * normed, axis=0, keepdims=True)
        grads[pl.ds(J + j, 1), :] = jnp.sum(lifted_grad, axis=0, keepdims=True)
        n_grad = lifted_grad * par[pl.ds(j, 1), :]
        rows_grad = factor * (
            n_grad
            - jnp.mean(n_grad, axis=1, keepdims=True)
            - normed * jnp.mean(n_grad * normed, axis=1, keepdims=True)
        )
        rows_grad = rows_grad.astype(BF16).astype(F32)
        xg[j, 1] = (xg[j, 1].astype(F32) + score_grad * par[pl.ds(2 * J + j, 1), :] + rows_grad).astype(BF16)
        send_home(1, j)
        return 0

    last = jnp.maximum(z, H - 1 - z)

    def item(q, _):
        s, j = q // J, q % J
        for up in (1, 0):
            chunk = z - s if up else z + s
            there = (chunk >= 0) if up else (chunk < H)

            @pl.when(jnp.logical_and(s > 0, there))
            def _(chunk=chunk, up=up):
                for a in range(2):
                    def pass_on(size, a=a):
                        gat_copy(a, j, chunk, up, size).wait_recv()
                        send_gat(a, j, chunk, up, size)

                    with_rows(chunk, pass_on)

        def side(d, _):
            chunk = jnp.where(d == 0, z - s, z + s)
            there = jnp.logical_and(jnp.logical_and(chunk >= 0, chunk < H), jnp.logical_or(s > 0, d == 0))

            @pl.when(there)
            def _():
                home = jnp.clip(chunk, 0, H - 1)
                compute(home, j)

                @pl.when(jnp.logical_and(s > 0, jnp.where(d == 0, z == H - 1, z == 0)))
                def _():
                    def begin(size):
                        for a in range(2):
                            for half in range(HALVES):
                                red_copy(a, j, half, home, d, size).start()

                    with_rows(home, begin)

            return 0

        lax.fori_loop(0, 2, side, 0)

        @pl.when(s > 0)
        def _():
            for a in range(2):
                for half in range(HALVES):

                    def through(k, _, a=a, half=half):
                        up = (k + jnp.where(z >= H // 2, 0, 1)) % 2
                        home = jnp.where(up == 1, s, H - 1 - s)
                        passes = jnp.where(
                            up == 1, jnp.logical_and(z > 0, z < home), jnp.logical_and(z < H - 1, z > home)
                        )

                        @pl.when(passes)
                        def _():
                            def add(size):
                                red_in(a, j, half, home, size).wait_recv()
                                at = (a, j, home, pl.ds(0, size), pl.ds(half * DH, DH))
                                sbuf[at] = (sbuf[at].astype(F32) + rbuf[at].astype(F32)).astype(BF16)
                                red_copy(a, j, half, home, up, size).start()

                            with_rows(home, add)

                        return 0

                    lax.fori_loop(0, 2, through, 0)

        @pl.when(q == J - 1)
        def _():
            for d in range(1, H):
                zs_copy(d, (z - d + H) % H).wait_recv()
            both = zs[0]
            for h in range(1, H):
                both = both + zs[h]
            mg[e] = both[0:8] / jnp.maximum(both[8:16], 1.0)
            for d in range(1, G):
                mg_copy(d, e).start()

        @pl.when(jnp.logical_and(s == last, j == J - 1))
        def _():
            for copy in outs:
                copy.start()
            lax.fori_loop(0, J, finish, 0)
            for d in range(1, H):
                gb_copy(d, z, (z + d) % H).start()

        return 0

    lax.fori_loop(0, H * J, item, 0)

    gbuf[z] = grads[:, own_cols]
    for d in range(1, G):
        mg_copy(d, (e - d + G) % G).wait_recv()
    means = jnp.zeros((8, 128), F32)
    for k in range(G):
        v = mg[k] if k == 0 else pltpu.roll(mg[k], k * J, 1)
        means = jnp.where((lane8 >= k * J) & (lane8 < k * J + J), v, means)
    o_mean[...] = means

    for d in range(1, H):
        gb_copy(d, (z - d + H) % H, z).wait_recv()
    small = gbuf[0]
    for h in range(1, H):
        small = small + gbuf[h]
    o_small[...] = small

    for d in range(1, H):
        par_copy(d, z).wait_send()
        zs_copy(d, z).wait_send()
        gb_copy(d, z, (z + d) % H).wait_send()
    for d in range(1, G):
        mg_copy(d, e).wait_send()
        for j in range(J):
            for a in range(2):
                disp_copy(j, a, d, (e + d) % G).wait_send()

    def drain(i, _):
        a, j, h = i // (J * H), i // H % J, i % H

        def wait(size):
            @pl.when(jnp.logical_and(z < H - 1, h <= z))
            def _():
                gat_copy(a, j, h, 1, size).wait_send()

            @pl.when(jnp.logical_and(z > 0, h >= z))
            def _():
                gat_copy(a, j, h, 0, size).wait_send()

            @pl.when(h != z)
            def _():
                for half in range(HALVES):
                    red_copy(a, j, half, h, jnp.where(h > z, 1, 0), size).wait_send()

        with_rows(h, wait)
        return 0

    lax.fori_loop(0, 2 * J * H, drain, 0)
    for copy in outs:
        copy.wait()
    for j in range(J):
        for a in range(2):
            ret_own(j, a).wait()
            for d in range(1, G):
                ret_copy(j, a, d, (e + d) % G).wait_send()
                ret_in(j, a, d).wait_recv()


def local_kernel(
    dims,
    gat, pg, act, ret, slot, tok, cot, small, bg, mean,
    o_mixed, o_tg, o_cent, o_gain, o_bias, o_win, o_bin, o_wout, o_bout, o_mean,
    v_gat, v_pg, v_act, v_ret, v_tok, v_cot, turned, v_win, v_wout, v_mixed, v_tg, in_sem, out_sem,
):
    G, H, J, S, MSG, R, T, D, F, PW, seq_len = dims
    parts = D // TILE
    n = J * G * MSG
    loads = {}
    for j in range(J):
        for name, a, b in (
            ("lift", gat.at[0, j], v_gat.at[0, j]), ("pg", pg.at[j], v_pg.at[j]),
            ("act", act.at[j], v_act.at[j]), ("grad", gat.at[1, j], v_gat.at[1, j]),
        ):
            loads[name, j] = pltpu.make_async_copy(a, b, in_sem.at[len(loads)])
    for name, a, b in (("ret", ret, v_ret), ("tok", tok, v_tok), ("cot", cot, v_cot)):
        loads[name] = pltpu.make_async_copy(a, b, in_sem.at[len(loads)])
    for copy in loads.values():
        copy.start()

    o_gain[...] = small[pl.ds(0, J), :]
    o_bias[...] = small[pl.ds(J, J), :]
    o_cent[...] = small[pl.ds(2 * J, J), :]
    o_bout[...] = small[pl.ds(3 * J, J), :]
    o_bin[...] = bg[...]
    o_mean[...] = mean[pl.ds(0, 1), pl.ds(0, G * J)]

    stores = []

    def outer(left, right, where, to, width):
        turned[pl.ds(0, left.shape[1]), :] = jnp.transpose(left)

        def tile(t, _):
            at = pl.ds(pl.multiple_of(t * TILE, TILE), TILE)
            where[:, at] = contract(turned[pl.ds(0, left.shape[1]), :], right[:, at])
            return 0

        lax.fori_loop(0, width // TILE, tile, 0)
        stores.append(pltpu.make_async_copy(where, to, out_sem.at[len(stores)]))
        stores[-1].start()

    for j in range(J):
        loads["lift", j].wait()
        loads["pg", j].wait()
        outer(v_gat[0, j], v_pg.at[j], v_win.at[j], o_win.at[j], F)
        loads["act", j].wait()
        loads["grad", j].wait()
        outer(v_act[j], v_gat.at[1, j], v_wout.at[j], o_wout.at[j], D)

    for name in ("ret", "tok", "cot"):
        loads[name].wait()
    turned_slot = jnp.transpose(jnp.broadcast_to(slot[pl.ds(0, 1), :].astype(F32), (128, T)))
    spot = turned_slot[:, 0:1].astype(jnp.int32)
    live = spot >= 0
    m = iota((T, n), 1)
    for part in range(parts):
        at = pl.ds(part * TILE, TILE)
        take = ones_where(spot + part * S == m)
        v = contract(take, v_ret[0])
        v_mixed[:, at] = jnp.where(live, v, v_tok[:, at].astype(F32)).astype(BF16)
        w = contract(take, v_ret[1])
        v_tg[:, at] = jnp.where(live, w, v_cot[:, at].astype(F32)).astype(BF16)
    for a, b in ((v_mixed, o_mixed), (v_tg, o_tg)):
        stores.append(pltpu.make_async_copy(a, b, out_sem.at[len(stores)]))
        stores[-1].start()
    for copy in stores:
        copy.wait()


def on_device(
    tokens, assignment, lengths, centroids, ln_gain, ln_bias, w_in, b_in, w_out, b_out, cotangent
):
    T, D = tokens.shape
    G, H = lax.axis_size("expert"), lax.axis_size("hidden")
    J, F = w_in.shape[0], w_in.shape[2]
    PW = centroids.shape[1]
    S = max(2, 9 * T // (8 * J * G))
    parts = D // TILE
    MSG = -(-(parts * S + 1) // 16) * 16
    R, GM = G * S, G * MSG
    seq_len = min(2048, H * T)
    dims = (G, H, J, S, MSG, R, T, D, F, PW, seq_len)
    vm = pl.BlockSpec(memory_space=pltpu.VMEM)
    hbm = pl.BlockSpec(memory_space=pl.ANY)
    sm = pl.BlockSpec(memory_space=pltpu.SMEM)
    dma = pltpu.SemaphoreType.DMA
    shape = jax.ShapeDtypeStruct

    def exchange(number, sizes, *args):
        return pl.pallas_call(
            functools.partial(exchange_kernel, dims, sizes),
            name="exchange",
            out_shape=[
                shape((2, J, H, R, D), BF16),
                shape((J, H, R, F), BF16),
                shape((J, H, R, F), BF16),
                shape((2, J, GM, TILE), BF16),
                shape((8, T), jnp.int32),
                shape((4 * J, PW), F32),
                shape((J, F), F32),
                shape((8, 128), F32),
            ],
            in_specs=[vm, sm, vm, vm, vm, vm, vm, hbm, hbm, hbm, hbm],
            out_specs=[hbm, hbm, hbm, hbm, vm, vm, vm, vm],
            scratch_shapes=[
                pltpu.VMEM((T, D), BF16),
                pltpu.VMEM((T, D), BF16),
                pltpu.VMEM((J, D, F), BF16),
                pltpu.VMEM((J, F, D), BF16),
                pltpu.VMEM((2, J, H, R, D), BF16),
                pltpu.VMEM((J, H, R, F), BF16),
                pltpu.VMEM((J, H, R, F), BF16),
                pltpu.VMEM((2, J, H, R, D), BF16),
                pltpu.VMEM((2, J, H + 1, R, D), BF16),
                pltpu.VMEM((J, 2, GM, TILE), BF16),
                pltpu.VMEM((J, 2, GM, TILE), BF16),
                pltpu.VMEM((2, J, GM, TILE), BF16),
                pltpu.VMEM((J, 2, R, D), BF16),
                pltpu.VMEM((parts, GM, T), BF16),
                pltpu.VMEM((parts, R, GM), BF16),
                pltpu.VMEM((parts, GM, R), BF16),
                pltpu.VMEM((R, GM), BF16),
                pltpu.VMEM((4 * J, D), F32),
                pltpu.VMEM((4, J, R, 1), F32),
                pltpu.VMEM((H, 16, 128), F32),
                pltpu.VMEM((G, 8, 128), F32),
                pltpu.VMEM((4 * J, D), F32),
                pltpu.VMEM((H, 4 * J, PW), F32),
                pltpu.VMEM((J, R, D), F32),
                dma((4,)),
                dma((H,)), dma((H,)),
                dma((H,)), dma((H,)),
                dma((G,)), dma((G,)),
                dma((H,)), dma((H,)),
                dma((J, 2, G)), dma((J, 2, G)),
                dma((J, 2, G)), dma((J, 2, G)),
                dma((2, 2, J, H)), dma((2, J, H)),
                dma((2, J, HALVES, H)), dma((2, J, HALVES, H + 1)),
                dma((3 + 2 * J,)),
            ],
            compiler_params=pltpu.CompilerParams(
                collective_id=number, has_side_effects=True, vmem_limit_bytes=60 * 2**20
            ),
            cost_estimate=pl.CostEstimate(
                flops=8 * J * H * R * D * F, bytes_accessed=30 * 2**20, transcendentals=J * H * R * F
            ),
        )(*args)

    args = (
        assignment.reshape(1, T), lengths, centroids, ln_gain, ln_bias, b_out, b_in, tokens, cotangent, w_in, w_out
    )
    options = []
    for shares in SHAPES:
        rows = [-(-G * shares[4 * h // H] // 8) * S for h in range(H)]
        options.append([-(-r // 16) * 16 for r in rows])
    if len(options) == 1:
        found = exchange(0, tuple(options[0]), *args)
    else:
        first = (jnp.arange(G, dtype=jnp.int32)[:, None] * H + jnp.arange(H, dtype=jnp.int32)[None, :]) * T
        needed = S * jnp.sum((lengths[first // seq_len] > first % seq_len).astype(jnp.int32), axis=0)
        fits = jnp.all(needed[None, :] <= jnp.asarray(options, jnp.int32), axis=1)
        which = jnp.max(jnp.where(fits, jnp.arange(len(options), dtype=jnp.int32), 0))
        def choose(low, high):
            if high - low == 1:
                return functools.partial(exchange, low, tuple(options[low]))
            middle = (low + high) // 2
            return lambda *args: lax.cond(which >= middle, choose(middle, high), choose(low, middle), *args)

        found = choose(0, len(options))(*args)
    gat, act, pg, ret, slot, small, bg, mean = found

    N = H * R
    outs = pl.pallas_call(
        functools.partial(local_kernel, dims),
        name="gradients",
        out_shape=[
            shape((T, D), BF16),
            shape((T, D), BF16),
            shape((J, PW), F32),
            shape((J, PW), F32),
            shape((J, PW), F32),
            shape((J, D, F), F32),
            shape((J, F), F32),
            shape((J, F, D), F32),
            shape((J, PW), F32),
            shape((1, G * J), F32),
        ],
        in_specs=[hbm, hbm, hbm, hbm, vm, hbm, hbm, vm, vm, vm],
        out_specs=[hbm, hbm, vm, vm, vm, hbm, vm, hbm, vm, vm],
        scratch_shapes=[
            pltpu.VMEM((2, J, N, D), BF16),
            pltpu.VMEM((J, N, F), BF16),
            pltpu.VMEM((J, N, F), BF16),
            pltpu.VMEM((2, J * GM, TILE), BF16),
            pltpu.VMEM((T, D), BF16),
            pltpu.VMEM((T, D), BF16),
            pltpu.VMEM((max(D, F), N), BF16),
            pltpu.VMEM((J, D, F), F32),
            pltpu.VMEM((J, F, D), F32),
            pltpu.VMEM((T, D), BF16),
            pltpu.VMEM((T, D), BF16),
            dma((4 * J + 3,)),
            dma((2 * J + 2,)),
        ],
        compiler_params=pltpu.CompilerParams(vmem_limit_bytes=60 * 2**20),
        cost_estimate=pl.CostEstimate(
            flops=4 * J * N * D * F, bytes_accessed=28 * 2**20, transcendentals=0
        ),
    )(
        gat.reshape(2, J, N, D), pg.reshape(J, N, F), act.reshape(J, N, F), ret.reshape(2, J * GM, TILE),
        slot, tokens, cotangent, small, bg, mean,
    )
    return (*outs[:9], outs[9].reshape(G * J))


def solution(mesh):
    tok = P(("expert", "hidden"), None)
    par = P("expert", "hidden")
    win = P("expert", None, "hidden")
    wout = P("expert", "hidden", None)
    return jax.shard_map(
        on_device,
        mesh=mesh,
        in_specs=(tok, tok, P(), par, par, par, win, par, wout, par, tok),
        out_specs=(tok, tok, par, par, par, win, par, wout, par, P()),
        check_vma=False,
    )
```

time: 190 us -> 160 us (0.84)
  the two profiles are of different devices: /device:TPU:11 before, /device:TPU:0 now
where the time goes in v2:
time: 160 us
  Pallas kernels  155 us (97%)
  between operations  1.66 us (1%)
    pallas_call x1, Pallas kernels, exchange(): pl.pallas_call(functools.partial(exchange_kernel, dims, sizes), name='exc...  139 us
    pallas_call x1, Pallas kernels, on_device(): pl.pallas_call(functools.partial(local_kernel, dims), name='gradients', o...  15.9 us

profile of v2, /device:TPU:0, one launch (start us, length us, event | category | flops | bytes accessed | tf_op | source)
XLA Modules:
  0.0 159.6 jit_solution(9345705740114994708)
XLA Ops:
  0.6 0.0 copy-start.1
  0.7 0.0 copy-start
  0.7 0.0 copy-start.3
  0.7 0.0 copy-start.2
  0.7 0.0 copy-start.7
  0.7 0.0 copy-start.4
  0.7 0.0 copy-start.6
  0.7 0.0 copy-start.5
  0.7 0.0 copy-start.9
  0.7 0.0 copy-start.8
  0.8 0.1 compare_select_fusion
  0.8 0.1 reshape.149
  0.9 0.4 copy-done
  1.3 0.7 gather_fusion
  2.0 0.1 reshape.148
  2.1 0.1 convert_reduce_fusion
  2.2 0.0 copy-done.1
  2.2 0.1 compare_reduce_fusion
  2.3 0.6 select_reduce_fusion
  3.6 0.0 copy-done.3
  3.6 0.0 copy-done.2
  3.7 0.0 copy-done.7
  3.7 0.0 copy-done.4
  3.7 0.0 copy-done.6
  3.7 0.0 copy-done.5
  3.7 0.0 copy-done.9
  3.7 0.0 copy-done.8
  3.7 139.8 %conditional.1 = ((bf16[2,2,4,144,1024]{4,3,2,1,0:T(8,128)(2,1)}, bf16[2,4,144,1024]{3,2,1,0:T(8,128)(2,1)S(1)}, bf16[2,4,144,1024]{3,2,1,0:T(8,128)(2,1)}, bf16...) conditional(s32[]{:T(128)} %convert_element_type.7, ...), branch_computations={%region_3.4_spmd, %region_4.5_spmd} | conditional | flops 9663676416 | bytes 31457288 | solution.py:698
  3.9 139.4 %exchange.3 = (bf16[2,2,4,144,1024]{4,3,2,1,0:T(8,128)(2,1)}, bf16[2,4,144,1024]{3,2,1,0:T(8,128)(2,1)S(1)}, bf16[2,4,144,1024]{3,2,1,0:T(8,128)(2,1)}, bf16[2,2...) custom-call(s32[1,256]{1,0:T(1,128)S(1)} %get-tuple-element.84.asg, ...), custom_call_target="tpu_custom_call" | custom-call | flops 9663676416 | bytes 31457280 | tf_op jit(solution)/shard_map/cond/branch_1_fun/exchange/pallas_call | solution.py:621
  143.5 15.9 %gradients.1 = (bf16[256,1024]{1,0:T(8,128)(2,1)}, bf16[256,1024]{1,0:T(8,128)(2,1)}, f32[2,256]{1,0:T(2,128)}, f32[2,256]{1,0:T(2,128)}, f32[2,256]{1,0:T(2,128...) custom-call(bf16[2,2,576,1024]{3,2,1,0:T(8,128)(2,1)} %bitcast.10, ...), custom_call_target="tpu_custom_call" | custom-call | flops 4831838208 | bytes 29360128 | tf_op jit(solution)/shard_map/gradients/pallas_call | solution.py:704
  (3 shorter events, 0.0 us)
Async XLA Ops:
  0.6 1.6 copy-start.1
  0.7 0.7 copy-start
  0.7 3.0 %copy-start.3 = (bf16[256,1024]{1,0:T(8,128)(2,1)S(1)}, bf16[256,1024]{1,0:T(8,128)(2,1)}, u32[]{:S(2)}) copy-start(bf16[256,1024]{1,0:T(8,128)(2,1)} %cot.1) | copy-start | bytes 1572868
  0.7 3.0 %copy-start.2 = (bf16[256,1024]{1,0:T(8,128)(2,1)S(1)}, bf16[256,1024]{1,0:T(8,128)(2,1)}, u32[]{:S(2)}) copy-start(bf16[256,1024]{1,0:T(8,128)(2,1)} %tok.1) | copy-start | bytes 1572868
  0.7 3.0 %copy-start.7 = (f32[2,256]{1,0:T(2,128)S(1)}, f32[2,256]{1,0:T(2,128)}, u32[]{:S(2)}) copy-start(f32[2,256]{1,0:T(2,128)} %param.23) | copy-start | bytes 6148
  0.7 3.0 %copy-start.4 = (f32[2,1024]{1,0:T(2,128)S(1)}, f32[2,1024]{1,0:T(2,128)}, u32[]{:S(2)}) copy-start(f32[2,1024]{1,0:T(2,128)} %param.21) | copy-start | bytes 24580
  0.7 3.0 %copy-start.6 = (f32[2,256]{1,0:T(2,128)S(1)}, f32[2,256]{1,0:T(2,128)}, u32[]{:S(2)}) copy-start(f32[2,256]{1,0:T(2,128)} %param.19) | copy-start | bytes 6148
  0.7 3.0 %copy-start.5 = (f32[2,256]{1,0:T(2,128)S(1)}, f32[2,256]{1,0:T(2,128)}, u32[]{:S(2)}) copy-start(f32[2,256]{1,0:T(2,128)} %param.18) | copy-start | bytes 6148
  0.7 3.0 %copy-start.9 = (bf16[2,256]{1,0:T(2,128)(2,1)S(1)}, bf16[2,256]{1,0:T(2,128)(2,1)}, u32[]{:S(2)}) copy-start(bf16[2,256]{1,0:T(2,128)(2,1)} %param.17) | copy-start | bytes 3076
  0.7 3.0 %copy-start.8 = (s32[256,1]{0,1:T(1,128)S(1)}, s32[256,1]{0,1:T(1,128)}, u32[]{:S(2)}) copy-start(s32[256,1]{0,1:T(1,128)} %param.15) | copy-start | bytes 3076

commit v3 on v2

v3 whole, which is shorter than its diff:
```python
import functools

import jax
import jax.numpy as jnp
from jax import lax
from jax.experimental import pallas as pl
from jax.experimental.pallas import tpu as pltpu
from jax.sharding import PartitionSpec as P

EPS = 1e-05
MESH = pl.DeviceIdType.MESH
F32 = jnp.float32
BF16 = jnp.bfloat16
TILE = 256
HALVES = 2
GELU_A = 0.7978845608028654
GELU_B = 0.044715
SHAPES = ((8, 8, 8, 8), (8, 7, 5, 4), (8, 6, 4, 3),)


def contract(a, b, dims=((1,), (0,))):
    return lax.dot_general(a, b, (dims, ((), ())), preferred_element_type=F32)


def iota(shape, axis):
    return lax.broadcasted_iota(jnp.int32, shape, axis)


def ones_where(mask):
    return mask.astype(F32).astype(BF16)


def per(index, size, count):
    return jnp.floor((index.astype(F32) + 0.5) * (1.0 / size)).astype(jnp.int32)


def layer_kernel(
    dims, sizes,
    asg, lens, cent, gain, bias, bout, bin_, tok_in, cot_in, win, wout,
    home, ret, o_slot, o_cent, o_gain, o_bias, o_win, o_bin, o_wout, o_bout, o_mean,
    vwin, vwout, gat, act, pg, sbuf, rbuf, snd, rcv, xg, spread, pick, unpick, pick_count,
    par, stats, zs, mg, grads, gbuf, normed_of, turned,
    w_sem, par_s, par_r, zs_s, zs_r, mg_s, mg_r, gb_s, gb_r,
    disp_s, disp_r, ret_s, ret_r, gat_s, gat_r, red_s, red_r,
):
    G, H, J, S, MSG, R, T, D, F, PW, seq_len = dims
    e, z = lax.axis_index("expert"), lax.axis_index("hidden")
    E, GM, N = G * J, G * MSG, H * R
    parts, ftiles = D // TILE, F // TILE
    BLOCK = R

    def cols(t, size=TILE):
        return pl.ds(pl.multiple_of(t * size, size), size)

    def rows(start, size):
        return pl.ds(pl.multiple_of(start, 16), size)

    def loop(count, body):
        def step(i, _):
            body(i)
            return 0

        lax.fori_loop(0, count, step, 0)

    barrier = pltpu.get_barrier_semaphore()
    for d in range(1, H):
        pl.semaphore_signal(barrier, inc=1, device_id=(e, (z + d) % H), device_id_type=MESH)
    for d in range(1, G):
        pl.semaphore_signal(barrier, inc=1, device_id=((e + d) % G, z), device_id_type=MESH)

    loads = []
    for a, source in enumerate((tok_in, cot_in)):
        for part in range(parts):
            loads.append(pltpu.make_async_copy(
                source.at[:, pl.ds(part * TILE, TILE)], home.at[a, pl.ds(part * T, T), :],
                w_sem.at[a * parts + part]))
    weights = [
        pltpu.make_async_copy(win, vwin, w_sem.at[2 * parts]),
        pltpu.make_async_copy(wout, vwout, w_sem.at[2 * parts + 1]),
    ]
    for copy in loads + weights:
        copy.start()

    own_cols = cols(z, PW)
    par[pl.ds(0, J), own_cols] = gain[...]
    par[pl.ds(J, J), own_cols] = bias[...]
    par[pl.ds(2 * J, J), own_cols] = cent[...].astype(F32)
    par[pl.ds(3 * J, J), own_cols] = bout[...]

    expert = asg[...]
    place = (e * H + z) * T
    length = lens[place // seq_len]
    live = (place % seq_len + iota((1, T), 1)) < length
    sub_e = iota((E, 1), 0)
    hot = ((expert == sub_e) & live).astype(F32)
    earlier = ones_where(iota((T, T), 0) < iota((T, T), 1))
    before = contract(hot.astype(BF16), earlier)
    group = per(sub_e, J, G)
    inner = sub_e - group * J
    rank = jnp.sum(hot * before, axis=0, keepdims=True).astype(jnp.int32)
    to_group = jnp.sum(hot * group.astype(F32), axis=0, keepdims=True).astype(jnp.int32)
    to_inner = jnp.sum(hot * inner.astype(F32), axis=0, keepdims=True).astype(jnp.int32)
    to_inner = jnp.where(live, to_inner, -1)
    message = to_group * MSG
    o_slot[...] = jnp.broadcast_to(jnp.where(live, to_inner * GM + message + rank, -D * D), (8, T))

    pl.semaphore_wait(barrier, (H - 1) + (G - 1))

    def par_copy(d, source):
        return pltpu.make_async_remote_copy(
            src_ref=par.at[:, cols(source, PW)], dst_ref=par.at[:, cols(source, PW)],
            send_sem=par_s.at[d], recv_sem=par_r.at[d],
            device_id=(e, (z + d) % H), device_id_type=MESH)

    for d in range(1, H):
        par_copy(d, z).start()

    def msg(k):
        return pl.ds(pl.multiple_of(k * MSG, MSG), MSG)

    def disp_copy(j, a, d, target):
        return pltpu.make_async_remote_copy(
            src_ref=snd.at[j, a, msg(target)], dst_ref=rcv.at[j, a, msg(e)],
            send_sem=disp_s.at[j, a, d], recv_sem=disp_r.at[j, a, d],
            device_id=(target, z), device_id_type=MESH)

    def disp_in(j, a, d):
        k = (e - d + G) % G
        return pltpu.make_async_remote_copy(
            src_ref=snd.at[j, a, msg(k)], dst_ref=rcv.at[j, a, msg(k)],
            send_sem=disp_s.at[j, a, d], recv_sem=disp_r.at[j, a, d],
            device_id=((e + d) % G, z), device_id_type=MESH)

    def dispatch(i):
        j, a = i // 2, i % 2
        row = iota((GM, T), 0)
        mine = to_inner == j

        @pl.when(a == 0)
        def _():
            at = jnp.where(mine, message + rank, -D * D)
            for part in range(parts):
                spread[:, pl.ds(part * T, T)] = ones_where(at + part * S == row)

        for b in range(2):
            @pl.when(jnp.logical_and(j == 0, a == b))
            def _(b=b):
                for copy in loads[b * parts:(b + 1) * parts]:
                    copy.wait()

        counted = jnp.where(mine & (a == 0), message + parts * S, -1)
        v = contract(spread[...], home[a]) + contract(ones_where(counted == row), jnp.ones((T, TILE), BF16))
        snd[j, a] = v.astype(BF16)
        for d in range(1, G):
            disp_copy(j, a, d, (e + d) % G).start()
        rcv[j, a, msg(e), :] = snd[j, a, msg(e), :]

    loop(2 * J, dispatch)

    def row_of(c):
        k = per(c, MSG, G)
        start = jnp.full(c.shape, -D * D, jnp.int32)
        filled_before = jnp.int32(0)
        for i in range(G):
            first = (i * H + z) * T
            some = lens[first // seq_len] > first % seq_len
            start = jnp.where((k == i) & some, filled_before * S, start)
            filled_before = filled_before + some.astype(jnp.int32)
        return start, c - k * MSG

    start, within = row_of(iota((1, GM), 1))
    down = iota((R, GM), 0)
    for part in range(parts):
        i = within - part * S
        pick[pl.ds(part * R, R), :] = ones_where(jnp.where((i >= 0) & (i < S), start + i, -1) == down)
    counts_at = jnp.where(within == parts * S, start, -D * D)
    pick_count[...] = ones_where((down >= counts_at) & (down < counts_at + S))
    start, within = row_of(iota((GM, 1), 0))
    across = iota((1, parts * R), 1)
    across_part = per(across, R, parts)
    i = within - across_part * S
    unpick[...] = ones_where((i >= 0) & (i < S) & (start + i == across - across_part * R))

    for h in range(H):
        if sizes[h] < R:
            gat[:, :, pl.ds(h * R + sizes[h], R - sizes[h]), :] = jnp.zeros((2, J, R - sizes[h], D), BF16)

    def clear(slot_at):
        def one(i):
            rbuf[i // J, i % J, slot_at] = jnp.zeros((R, D), BF16)

        loop(2 * J, one)

    pl.when(z == 0)(lambda: clear(H))
    pl.when(z == H - 1)(lambda: clear(H - 1))

    o_bin[...] = jnp.zeros_like(o_bin)

    for d in range(1, H):
        par_copy(d, (z - d + H) % H).wait_recv()

    def with_rows(chunk, body):
        for size in sorted(set(sizes)):
            planes = [h for h in range(H) if sizes[h] == size]
            if len(planes) == H:
                body(size)
            else:
                hit = chunk == planes[0]
                for h in planes[1:]:
                    hit = jnp.logical_or(hit, chunk == h)
                pl.when(hit)(functools.partial(body, size))

    def gat_copy(a, j, chunk, up, size):
        at = (a, j, rows(chunk * R, size))
        return pltpu.make_async_remote_copy(
            src_ref=gat.at[at], dst_ref=gat.at[at],
            send_sem=gat_s.at[up, a, j, chunk], recv_sem=gat_r.at[a, j, chunk],
            device_id=(e, jnp.clip(z + 2 * up - 1, 0, H - 1)), device_id_type=MESH)

    def send_gat(a, j, chunk, up, size):
        @pl.when(jnp.where(up == 1, z < H - 1, z > 0))
        def _():
            gat_copy(a, j, chunk, up, size).start()

    def send_own(a, j):
        def both(size):
            send_gat(a, j, z, 1, size)
            send_gat(a, j, z, 0, size)

        with_rows(z, both)

    def half_of(size, half):
        first = -(-size // 32) * 16
        return (0, first) if half == 0 else (first, size - first)

    def red_copy(a, j, half, to, up, size):
        slot_to = jnp.where(jnp.logical_and(up == 1, to == z + 1), H, to)
        at = pl.ds(*half_of(size, half))
        return pltpu.make_async_remote_copy(
            src_ref=sbuf.at[a, j, to, at], dst_ref=rbuf.at[a, j, slot_to, at],
            send_sem=red_s.at[a, j, half, to], recv_sem=red_r.at[a, j, half, slot_to],
            device_id=(e, jnp.clip(z + 2 * up - 1, 0, H - 1)), device_id_type=MESH)

    def red_in(a, j, half, slot_at, size):
        at = pl.ds(*half_of(size, half))
        return pltpu.make_async_remote_copy(
            src_ref=sbuf.at[a, j, 0, at], dst_ref=rbuf.at[a, j, slot_at, at],
            send_sem=red_s.at[a, j, half, 0], recv_sem=red_r.at[a, j, half, slot_at],
            device_id=(e, jnp.clip(z + 1, 0, H - 1)), device_id_type=MESH)

    def quarter(part, b):
        return pl.ds(pl.multiple_of(part * R + b * BLOCK, 16), BLOCK)

    lane8 = iota((8, 128), 1)
    r1 = iota((R, 1), 0)
    rank_in = (r1 - S * per(r1, S, G)).astype(F32)
    zs[z] = jnp.zeros((16, 128), F32)

    def take_in(j, a):
        for d in range(1, G):
            disp_in(j, a, d).wait_recv()
        xg[j, a] = contract(pick[...], rcv[j, a]).astype(BF16)

    def prepare(j):
        take_in(j, 0)
        count = contract(pick_count[...], rcv[j, 0, :, pl.ds(0, 128)])[:, 0:1]
        stats[3, j] = (rank_in < count).astype(F32)

        def block(b):
            x = [xg[j, 0, quarter(part, b), :].astype(F32) for part in range(parts)]
            mean = sum(jnp.sum(v, axis=1, keepdims=True) for v in x) * (1.0 / D)
            x_mid = [v - mean for v in x]
            var = sum(jnp.sum(v * v, axis=1, keepdims=True) for v in x_mid) * (1.0 / D)
            factor = lax.rsqrt(var + EPS)
            score = 0.0
            at = rows(b * BLOCK, BLOCK)
            for part in range(parts):
                lanes = pl.ds(part * TILE, TILE)
                normed = x_mid[part] * factor
                lifted = normed * par[pl.ds(j, 1), lanes] + par[pl.ds(J + j, 1), lanes]
                gat[0, j, rows(z * R + b * BLOCK, BLOCK), lanes] = lifted.astype(BF16)
                normed_of[j, at, lanes] = normed
                score = score + jnp.sum(x[part] * par[pl.ds(2 * J + j, 1), lanes], axis=1, keepdims=True)
            stats[0, j, at] = jax.nn.sigmoid(score)
            stats[1, j, at] = factor

        loop(R // BLOCK, block)
        send_own(0, j)
        take_in(j, 1)

        def weigh(b):
            at = rows(b * BLOCK, BLOCK)
            for part in range(parts):
                g = xg[j, 1, quarter(part, b), :].astype(F32)
                gat[1, j, rows(z * R + b * BLOCK, BLOCK), pl.ds(part * TILE, TILE)] = (stats[0, j, at] * g).astype(BF16)

        loop(R // BLOCK, weigh)
        send_own(1, j)
        total = jnp.sum(stats[3, j] * stats[0, j], axis=0, keepdims=True)
        number = jnp.sum(stats[3, j], axis=0, keepdims=True)
        zs[z, pl.ds(0, 8), :] += jnp.where(lane8 == j, total, 0.0)
        zs[z, pl.ds(8, 8), :] += jnp.where(lane8 == j, number, 0.0)

    loop(J, prepare)

    def zs_copy(d, source):
        return pltpu.make_async_remote_copy(
            src_ref=zs.at[source], dst_ref=zs.at[source],
            send_sem=zs_s.at[d], recv_sem=zs_r.at[d],
            device_id=(e, (z + d) % H), device_id_type=MESH)

    for d in range(1, H):
        zs_copy(d, z).start()

    for copy in weights:
        copy.wait()

    def compute(chunk, j):
        mine = rows(chunk * R, R)

        def first(t):
            pre = contract(gat[0, j, mine, :], vwin[j, :, cols(t)]) + bin_[pl.ds(j, 1), cols(t)]
            sq = pre * pre
            th = jnp.tanh(pre * (GELU_A + (GELU_A * GELU_B) * sq))
            cdf = 0.5 + 0.5 * th
            slope = cdf + pre * (0.5 - 0.5 * th * th) * (GELU_A + (3.0 * GELU_A * GELU_B) * sq)
            act[j, mine, cols(t)] = (pre * cdf).astype(BF16)
            act_grad = contract(gat[1, j, mine, :], vwout[j, cols(t), :], ((1,), (1,)))
            pre_grad = (act_grad * slope).astype(BF16)
            pg[j, mine, cols(t)] = pre_grad
            o_bin[pl.ds(j, 1), cols(t)] += jnp.sum(pre_grad.astype(F32), axis=0, keepdims=True)

        loop(ftiles, first)

        def second(t):
            v = contract(act[j, mine, :], vwout[j, :, cols(t)])
            sbuf[0, j, chunk, :, cols(t)] = v.astype(BF16)
            w = contract(pg[j, mine, :], vwin[j, cols(t), :], ((1,), (1,)))
            sbuf[1, j, chunk, :, cols(t)] = w.astype(BF16)

        loop(parts, second)

    def outer(left, right, to, tall, wide):
        turned[pl.ds(0, tall), :] = jnp.transpose(left)

        def tile(t):
            to[:, cols(t)] = contract(turned[pl.ds(0, tall), :], right[:, cols(t)])

        loop(wide // TILE, tile)

    def mg_copy(d, source):
        return pltpu.make_async_remote_copy(
            src_ref=mg.at[source], dst_ref=mg.at[source],
            send_sem=mg_s.at[d], recv_sem=mg_r.at[d],
            device_id=((e + d) % G, z), device_id_type=MESH)

    def gb_copy(d, source, target):
        return pltpu.make_async_remote_copy(
            src_ref=grads.at[:, cols(target, PW)], dst_ref=gbuf.at[source],
            send_sem=gb_s.at[d], recv_sem=gb_r.at[d],
            device_id=(e, (z + d) % H), device_id_type=MESH)

    def ret_copy(j, a, d, target):
        return pltpu.make_async_remote_copy(
            src_ref=snd.at[j, a, msg(target)], dst_ref=ret.at[a, rows(j * GM + e * MSG, MSG)],
            send_sem=ret_s.at[j, a, d], recv_sem=ret_r.at[j, a, d],
            device_id=(target, z), device_id_type=MESH)

    def ret_in(j, a, d):
        k = (e - d + G) % G
        return pltpu.make_async_remote_copy(
            src_ref=snd.at[j, a, msg(k)], dst_ref=ret.at[a, rows(j * GM + k * MSG, MSG)],
            send_sem=ret_s.at[j, a, d], recv_sem=ret_r.at[j, a, d],
            device_id=((e + d) % G, z), device_id_type=MESH)

    def wait_sums(a, j):
        def both(size):
            for half in range(HALVES):
                @pl.when(z < H - 1)
                def _(half=half):
                    red_in(a, j, half, z, size).wait_recv()

                @pl.when(z > 0)
                def _(half=half):
                    red_in(a, j, half, H, size).wait_recv()

        with_rows(z, both)

    def summed(a, j, b, part):
        at = (rows(b * BLOCK, BLOCK), pl.ds(part * TILE, TILE))
        v = sbuf[(a, j, z, *at)].astype(F32) + rbuf[(a, j, z, *at)].astype(F32) + rbuf[(a, j, H, *at)].astype(F32)
        return jnp.where(stats[3, j, at[0]] > 0.5, v, 0.0)

    def send_home(j, a):
        snd[j, a] = contract(unpick[...], xg[j, a]).astype(BF16)
        for d in range(1, G):
            ret_copy(j, a, d, (e + d) % G).start()
        ret[a, rows(j * GM + e * MSG, MSG), :] = snd[j, a, msg(e), :]

    def finish(j):
        wait_sums(0, j)

        def forward(b):
            at = rows(b * BLOCK, BLOCK)
            gate = stats[0, j, at]
            gate_grad = 0.0
            for part in range(parts):
                lanes = pl.ds(part * TILE, TILE)
                branch = (summed(0, j, b, part) + par[pl.ds(3 * J + j, 1), lanes]).astype(BF16).astype(F32)
                x = xg[j, 0, quarter(part, b), :].astype(F32)
                gate_grad = gate_grad + jnp.sum(
                    xg[j, 1, quarter(part, b), :].astype(F32) * branch, axis=1, keepdims=True)
                rbuf[0, j, H, at, lanes] = x.astype(BF16)
                xg[j, 0, quarter(part, b), :] = (x + gate * branch).astype(BF16)
            score_grad = gate_grad * gate * (1.0 - gate)
            stats[2, j, at] = score_grad
            for part in range(parts):
                lanes = pl.ds(part * TILE, TILE)
                x = rbuf[0, j, H, at, lanes].astype(F32)
                grads[pl.ds(2 * J + j, 1), lanes] += jnp.sum(score_grad * x, axis=0, keepdims=True)
                sent = gat[1, j, rows(z * R + b * BLOCK, BLOCK), lanes].astype(F32)
                grads[pl.ds(3 * J + j, 1), lanes] += jnp.sum(sent, axis=0, keepdims=True)

        loop(R // BLOCK, forward)
        send_home(j, 0)
        wait_sums(1, j)

        def backward(b):
            at = rows(b * BLOCK, BLOCK)
            factor, score_grad = stats[1, j, at], stats[2, j, at]
            sum_n, sum_nn = 0.0, 0.0
            n_grads = []
            for part in range(parts):
                lanes = pl.ds(part * TILE, TILE)
                lifted_grad = summed(1, j, b, part)
                normed = normed_of[j, at, lanes]
                grads[pl.ds(j, 1), lanes] += jnp.sum(lifted_grad * normed, axis=0, keepdims=True)
                grads[pl.ds(J + j, 1), lanes] += jnp.sum(lifted_grad, axis=0, keepdims=True)
                n_grad = lifted_grad * par[pl.ds(j, 1), lanes]
                sum_n = sum_n + jnp.sum(n_grad, axis=1, keepdims=True)
                sum_nn = sum_nn + jnp.sum(n_grad * normed, axis=1, keepdims=True)
                n_grads.append(n_grad)
            for part in range(parts):
                lanes = pl.ds(part * TILE, TILE)
                rows_grad = factor * (
                    n_grads[part] - sum_n * (1.0 / D) - normed_of[j, at, lanes] * (sum_nn * (1.0 / D)))
                rows_grad = rows_grad.astype(BF16).astype(F32)
                g = xg[j, 1, quarter(part, b), :].astype(F32)
                moved = g + score_grad * par[pl.ds(2 * J + j, 1), lanes] + rows_grad
                xg[j, 1, quarter(part, b), :] = moved.astype(BF16)

        loop(R // BLOCK, backward)
        send_home(j, 1)

    last = jnp.maximum(z, H - 1 - z)
    grads[...] = jnp.zeros_like(grads)

    def sent(i):
        for d in range(1, G):
            disp_copy(i // 2, i % 2, d, (e + d) % G).wait_send()

    def starts(up):
        return jnp.where(up == 1, z == 0, z == H - 1)

    def passes(up, to):
        return jnp.where(up == 1, (z > 0) & (z < to), (z < H - 1) & (z > to))

    def begin(to, j, up):
        def both(size):
            for a in range(2):
                for half in range(HALVES):
                    red_copy(a, j, half, to, up, size).start()

        with_rows(to, both)

    def pass_sum(a, j, to, up):
        def both(size):
            for half in range(HALVES):
                red_in(a, j, half, to, size).wait_recv()
                at = (a, j, to, pl.ds(*half_of(size, half)))
                sbuf[at] = (sbuf[at].astype(F32) + rbuf[at].astype(F32)).astype(BF16)
                red_copy(a, j, half, to, up, size).start()

        with_rows(to, both)

    def item(q):
        s, j = q // J, q % J

        def forwarded(i):
            up, a = 1 - i // 2, i % 2
            chunk = jnp.where(up == 1, z - s, z + s)

            @pl.when((s > 0) & (chunk >= 0) & (chunk < H))
            def _():
                def pass_on(size):
                    gat_copy(a, j, chunk, up, size).wait_recv()
                    send_gat(a, j, chunk, up, size)

                with_rows(chunk, pass_on)

        loop(4, forwarded)

        def side(d):
            chunk = jnp.where(d == 0, z - s, z + s)

            @pl.when((chunk >= 0) & (chunk < H) & ((s > 0) | (d == 0)))
            def _():
                compute(chunk, j)

                @pl.when(starts(d) & (s > 0) & ((s > 1) | (j < J - 1)))
                def _():
                    begin(chunk, j, d)

        loop(2, side)

        early = (s == last + 1) & (s < H) & (j < J - 1)
        late = (s == H) & ((last == H - 1) | (j == J - 1))

        @pl.when((s == last + 1) & (j == 0))
        def _():
            loop(2 * J, sent)

        @pl.when(early | late)
        def _():
            finish(j)

        def through(i):
            a, up = i // 2, (i + jnp.where(z >= H // 2, 0, 1)) % 2
            to = jnp.where(up == 1, s, H - 1 - s)
            near = (to == z + 2 * up - 1) & (j == J - 1) & (s < H - 1)

            @pl.when((s > 0) & (s < H) & passes(up, to) & jnp.logical_not(near))
            def _():
                pass_sum(a, j, to, up)

        loop(4, through)

        @pl.when(q == H * J - 1)
        def _():
            for up in range(2):
                to = z + 2 * up - 1

                @pl.when(starts(up) & (to >= 0) & (to < H))
                def _(up=up, to=to):
                    begin(to, J - 1, up)

                @pl.when(passes(up, to) & (jnp.where(up == 1, to, H - 1 - to) < H - 1))
                def _(up=up, to=to):
                    loop(2, lambda a: pass_sum(a, J - 1, to, up))

        @pl.when(q == J - 1)
        def _():
            for d in range(1, H):
                zs_copy(d, (z - d + H) % H).wait_recv()
            both = zs[0]
            for h in range(1, H):
                both = both + zs[h]
            mg[e] = both[0:8] / jnp.maximum(both[8:16], 1.0)
            for d in range(1, G):
                mg_copy(d, e).start()

        @pl.when(s == last)
        def _():
            outer(gat[0, j], pg.at[j], o_win.at[j], D, F)
            outer(act[j], gat.at[1, j], o_wout.at[j], F, D)

    loop((H + 1) * J, item)
    for d in range(1, H):
        gb_copy(d, z, (z + d) % H).start()

    gbuf[z] = grads[:, own_cols]
    for d in range(1, G):
        mg_copy(d, (e - d + G) % G).wait_recv()
    means = jnp.zeros((8, 128), F32)
    for k in range(G):
        v = mg[k] if k == 0 else pltpu.roll(mg[k], k * J, 1)
        means = jnp.where((lane8 >= k * J) & (lane8 < k * J + J), v, means)
    o_mean[...] = means[0:1, 0:E]

    for d in range(1, H):
        gb_copy(d, (z - d + H) % H, z).wait_recv()
    small = gbuf[0]
    for h in range(1, H):
        small = small + gbuf[h]
    o_gain[...] = small[0:J]
    o_bias[...] = small[J:2 * J]
    o_cent[...] = small[2 * J:3 * J]
    o_bout[...] = small[3 * J:4 * J]

    for d in range(1, H):
        par_copy(d, z).wait_send()
        zs_copy(d, z).wait_send()
        gb_copy(d, z, (z + d) % H).wait_send()
    for d in range(1, G):
        mg_copy(d, e).wait_send()

    def drain(i):
        a, j, h = i // (J * H), i // H % J, i % H

        def wait(size):
            @pl.when((z < H - 1) & (h <= z))
            def _():
                gat_copy(a, j, h, 1, size).wait_send()

            @pl.when((z > 0) & (h >= z))
            def _():
                gat_copy(a, j, h, 0, size).wait_send()

            @pl.when(h != z)
            def _():
                for half in range(HALVES):
                    red_copy(a, j, half, h, jnp.where(h > z, 1, 0), size).wait_send()

        with_rows(h, wait)

    loop(2 * J * H, drain)

    def arrived(i):
        j, a = i // 2, i % 2
        for d in range(1, G):
            ret_in(j, a, d).wait_recv()
            ret_copy(j, a, d, (e + d) % G).wait_send()

    loop(2 * J, arrived)


def deliver_kernel(dims, home, ret, slot, *refs):
    G, H, J, S, MSG, R, T, D, F, PW, seq_len = dims
    results, (o_mixed, o_tg, *outs), (mixed, moved, sem) = refs[:8], refs[8:18], refs[18:]
    copies = [pltpu.make_async_copy(a, b, sem.at[i]) for i, (a, b) in enumerate(zip(results, outs))]
    for i in (3, 5, 0, 1, 2, 4, 6, 7):
        copies[i].start()

    spot = jnp.transpose(jnp.broadcast_to(slot[pl.ds(0, 1), :].astype(F32), (128, T)))[:, 0:1].astype(jnp.int32)
    live_rows = spot >= 0
    m = iota((T, J * G * MSG), 1)
    for part in range(D // TILE):
        take = ones_where(spot + part * S == m)
        at = pl.ds(part * TILE, TILE)
        for a, to in enumerate((mixed, moved)):
            kept = home[a, pl.ds(part * T, T), :].astype(F32)
            to[:, at] = jnp.where(live_rows, contract(take, ret[a]), kept).astype(BF16)
    for i, (a, b) in enumerate(((mixed, o_mixed), (moved, o_tg))):
        copies.append(pltpu.make_async_copy(a, b, sem.at[8 + i]))
        copies[-1].start()
    for copy in copies:
        copy.wait()


def on_device(
    tokens, assignment, lengths, centroids, ln_gain, ln_bias, w_in, b_in, w_out, b_out, cotangent
):
    T, D = tokens.shape
    G, H = lax.axis_size("expert"), lax.axis_size("hidden")
    J, F = w_in.shape[0], w_in.shape[2]
    PW = centroids.shape[1]
    S = max(2, 9 * T // (8 * J * G))
    parts = D // TILE
    MSG = -(-(parts * S + 1) // 16) * 16
    R, GM, N = G * S, G * MSG, H * G * S
    seq_len = min(2048, H * T)
    dims = (G, H, J, S, MSG, R, T, D, F, PW, seq_len)
    vm = pl.BlockSpec(memory_space=pltpu.VMEM)
    hbm = pl.BlockSpec(memory_space=pl.ANY)
    sm = pl.BlockSpec(memory_space=pltpu.SMEM)
    dma = pltpu.SemaphoreType.DMA
    buffers = [
        ((J, D, F), BF16),
        ((J, F, D), BF16),
        ((2, J, N, D), BF16),
        ((J, N, F), BF16),
        ((J, N, F), BF16),
        ((2, J, H, R, D), BF16),
        ((2, J, H + 1, R, D), BF16),
        ((J, 2, GM, TILE), BF16),
        ((J, 2, GM, TILE), BF16),
        ((J, 2, parts * R, TILE), BF16),
        ((GM, parts * T), BF16),
        ((parts * R, GM), BF16),
        ((GM, parts * R), BF16),
        ((R, GM), BF16),
        ((4 * J, D), F32),
        ((4, J, R, 1), F32),
        ((H, 16, 128), F32),
        ((G, 8, 128), F32),
        ((4 * J, D), F32),
        ((H, 4 * J, PW), F32),
        ((J, R, D), F32),
        ((max(D, F), N), BF16),
    ]
    taken = sum(
        jnp.dtype(t).itemsize * -(-s[-1] // 128) * 128 * functools.reduce(lambda a, b: a * b, s[:-1]) for s, t in buffers
    )

    results = [(J, PW), (J, PW), (J, PW), (J, D, F), (J, F), (J, F, D), (J, PW), (1, G * J)]
    shape = jax.ShapeDtypeStruct

    def layer(number, sizes, *args):
        made = pl.pallas_call(
            functools.partial(layer_kernel, dims, sizes),
            name="layer",
            out_shape=[
                pltpu.VMEM((2, parts * T, TILE), BF16),
                pltpu.VMEM((2, J * GM, TILE), BF16),
                pltpu.VMEM((8, T), jnp.int32),
                *[pltpu.VMEM(s, F32) for s in results],
            ],
            in_specs=[vm, sm, vm, vm, vm, vm, vm, hbm, hbm, hbm, hbm],
            out_specs=[vm] * 11,
            scratch_shapes=[
                *[pltpu.VMEM(s, t) for s, t in buffers],
                dma((2 * parts + 2,)),
                dma((H,)), dma((H,)),
                dma((H,)), dma((H,)),
                dma((G,)), dma((G,)),
                dma((H,)), dma((H,)),
                dma((J, 2, G)), dma((J, 2, G)),
                dma((J, 2, G)), dma((J, 2, G)),
                dma((2, 2, J, H)), dma((2, J, H)),
                dma((2, J, HALVES, H)), dma((2, J, HALVES, H + 1)),
            ],
            compiler_params=pltpu.CompilerParams(
                collective_id=number, has_side_effects=True, vmem_limit_bytes=taken + 3 * 2**20
            ),
            cost_estimate=pl.CostEstimate(
                flops=12 * J * N * D * F, bytes_accessed=30 * 2**20, transcendentals=J * N * F
            ),
        )(*args)
        return pl.pallas_call(
            functools.partial(deliver_kernel, dims),
            name="deliver",
            out_shape=[shape((T, D), BF16), shape((T, D), BF16), *[shape(s, F32) for s in results]],
            in_specs=[vm] * 11,
            out_specs=[hbm] * 10,
            scratch_shapes=[pltpu.VMEM((T, D), BF16), pltpu.VMEM((T, D), BF16), dma((10,))],
            compiler_params=pltpu.CompilerParams(vmem_limit_bytes=8 * 2**20),
        )(*made)

    args = (
        assignment.reshape(1, T), lengths, centroids, ln_gain, ln_bias, b_out, b_in, tokens, cotangent, w_in, w_out
    )
    options = []
    for shares in SHAPES:
        needed = [-(-G * shares[4 * h // H] // 8) * S for h in range(H)]
        options.append(tuple(-(-r // 16) * 16 for r in needed))
    if len(options) > 1:
        first = (jnp.arange(G, dtype=jnp.int32)[:, None] * H + jnp.arange(H, dtype=jnp.int32)[None, :]) * T
        if seq_len == H * T:
            lengths_of = lengths[:, None]
        else:
            lengths_of = lengths[first // seq_len]
        needed = S * jnp.sum((lengths_of > first % seq_len).astype(jnp.int32), axis=0)
        fits = jnp.all(needed[None, :] <= jnp.asarray(options, jnp.int32), axis=1)
        which = jnp.max(jnp.where(fits, jnp.arange(len(options), dtype=jnp.int32), 0))

    def choose(low, high):
        if high - low == 1:
            return functools.partial(layer, low, options[low])
        middle = (low + high) // 2
        return lambda *args: lax.cond(which >= middle, choose(middle, high), choose(low, middle), *args)

    outs = choose(0, len(options))(*args)
    return (*outs[:9], outs[9].reshape(G * J))


def solution(mesh):
    tok = P(("expert", "hidden"), None)
    par = P("expert", "hidden")
    win = P("expert", None, "hidden")
    wout = P("expert", "hidden", None)
    return jax.shard_map(
        on_device,
        mesh=mesh,
        in_specs=(tok, tok, P(), par, par, par, win, par, wout, par, tok),
        out_specs=(tok, tok, par, par, par, win, par, wout, par, P()),
        check_vma=False,
    )
```

time: 160 us -> 147 us (0.919)
  Pallas kernels: 155 us -> 142 us
    pallas_call x2, Pallas kernels: 155 us -> 142 us  [the longest x1 135 us: layer(): pl.pallas_call(functools.partial(layer_kernel, dims, sizes), name='layer'...]
where the time goes in v3:
time: 147 us
  Pallas kernels  142 us (97%)
  other arithmetic  2.26 us (2%)
  between operations  1.49 us (1%)
    pallas_call x1, Pallas kernels, layer(): pl.pallas_call(functools.partial(layer_kernel, dims, sizes), name='layer'...  135 us
    pallas_call x1, Pallas kernels, layer(): pl.pallas_call(functools.partial(deliver_kernel, dims), name='deliver', o...  6.36 us

profile of v3, /device:TPU:0, one launch (start us, length us, event | category | flops | bytes accessed | tf_op | source)
XLA Modules:
  0.0 146.7 jit_solution(15064164775556291812)
XLA Ops:
  0.7 0.8 convert_reduce_fusion
  1.4 0.8 compare_reduce_fusion
  2.2 0.7 select_reduce_fusion
  3.5 142.9 %conditional.2 = ((bf16[256,1024]{1,0:T(8,128)(2,1)}, bf16[256,1024]{1,0:T(8,128)(2,1)}, f32[2,256]{1,0:T(2,128)}, f32[2,256]{1,0:T(2,128)}, f32[2,256]{1,0:T(2,...) conditional(s32[]{:T(128)} %convert_element_type.10, ...), branch_computations={%region_3.4_spmd, %region_4.7_spmd} | conditional | flops 14495514624 | bytes 31457470 | solution.py:760
  4.2 142.0 %conditional = (bf16[256,1024]{1,0:T(8,128)(2,1)}, bf16[256,1024]{1,0:T(8,128)(2,1)}, f32[2,256]{1,0:T(2,128)}, f32[2,256]{1,0:T(2,128)}, f32[2,256]{1,0:T(2,128...) conditional(s32[]{:T(128)} %convert_element_type.6, ...), branch_computations={%region_5.5_spmd, %region_6.6_spmd} | conditional | flops 14495514624 | bytes 31457360 | solution.py:760
  4.4 135.2 %layer.4 = (bf16[2,1024,256]{2,1,0:T(8,128)(2,1)S(1)}, bf16[2,1280,256]{2,1,0:T(8,128)(2,1)S(1)}, s32[8,256]{1,0:T(8,128)S(1)}, f32[2,256]{1,0:T(2,128)S(1)}, f3...) custom-call(s32[1,256]{1,0:T(1,128)} %get-tuple-element.164.asg, ...), custom_call_target="tpu_custom_call" | custom-call | flops 14495514624 | bytes 31457280 | tf_op jit(solution)/shard_map/cond/branch_1_fun/cond/branch_0_fun/layer/pallas_call | solution.py:699
  139.6 6.4 %deliver.4 = (bf16[256,1024]{1,0:T(8,128)(2,1)}, bf16[256,1024]{1,0:T(8,128)(2,1)}, f32[2,256]{1,0:T(2,128)}, f32[2,256]{1,0:T(2,128)}, f32[2,256]{1,0:T(2,128)}...) custom-call(bf16[2,1024,256]{2,1,0:T(8,128)(2,1)S(1)} %get-tuple-ele, ...), custom_call_target="tpu_custom_call" | custom-call | tf_op jit(solution)/shard_map/cond/branch_1_fun/cond/branch_0_fun/deliver/pallas_call | solution.py:729
  (2 shorter events, 0.0 us)
